TPU v7x, 512 devices: a whole 4x4x16 slice. The times are simulated.
512 devices in a mesh: row: 32 (over x, y, core), col: 16 (over z).
Axes of the slice: x: 4, y: 4, z: 16, core: 2. Of those that a mesh axis runs over, the one named last changes fastest.
Arguments:
- left_blocks: float32 [2, 32, 32, 128, 128], P(None, 'row', 'col'), may hold values from -6 to 6
- left_index: int32 [2, 2, 32, 32], P(None, None, 'row', 'col'), may hold values from -1 to 31, as said below
- right_blocks: float32 [2, 32, 16, 128, 128], P(None, 'row', 'col'), may hold values from -0.5 to 0.5
- right_index: int32 [2, 2, 32, 16], P(None, None, 'row', 'col'), may hold values from -1 to 31, as said below
Outputs:
- product: float32 [16384, 8192], P('row', 'col')
Inputs may be any that keep to these rules, and one draw needn't show every extreme that they name: left_index[s, 0, r, t] is the block row within the band of 4 block rows, or -1 for an empty slot whose block is not used. left_index[s, 1, r, t] is a block column of the panel; slot t belongs to index t // 2 of col, which stores only the 32 / 16 block columns from (t // 2) * 32 / 16 on. The live slots of one device in one step name distinct blocks; in every step some device has all 2 slots live. right_index[s, 0, q, c] is a block row of the panel, or -1 for an empty slot whose block is not used; slot q belongs to index q // 1 of row, which stores only the 32 / 32 block rows from (q // 1) * 32 / 32 on. right_index[s, 1, q, c] is the block column within the band of 4. The live slots of one device in one step name distinct blocks; in every step some device has all 1 slots live.
All inputs are finite; a program needn't handle non-finite values.
Results may differ from a plain program's by a relative error of at most 0.0003.
Values sent between devices are 32-bit elements; how exact they have to be, the bound alone decides.
No kernel may reach another device: no remote copies, remote signals or barrier semaphores. Data moves between devices by JAX's collectives and lax.ppermute only.
A program may use at most 64 MiB of HBM per device.

v0:
```python
import jax
import jax.numpy as jnp
from jax import lax
from jax.sharding import PartitionSpec as P

BS = 128
PANEL = 32
STEPS = 2
BR = 4
BC = 4


precise_mode = lax.Precision.HIGHEST


def panel_product(
    left_part, left_where, right_part, right_where, capacity, owned_rows, row_span, col_span
):
    left_rows = left_where[0]
    left_cols = left_where[1]
    owners = left_cols // owned_rows
    picked = owners[:, None] * capacity + jnp.arange(capacity, dtype=jnp.int32)[None, :]
    right_pick = right_part[picked]
    right_rows = right_where[0][picked]
    right_cols = right_where[1][picked]
    matched = (right_rows == left_cols[:, None]) & (left_rows[:, None] >= 0)
    products = jnp.einsum("lab,lqbc->lqac", left_part, right_pick, precision=precise_mode)
    target = left_rows[:, None] * col_span + right_cols
    slots_out = jnp.arange(row_span * col_span, dtype=jnp.int32)
    placing = ((target[:, :, None] == slots_out[None, None, :]) & matched[:, :, None]).astype(
        jnp.float32
    )
    summed = jnp.einsum("lqac,lqn->nac", products, placing, precision=precise_mode)
    block_size = left_part.shape[1]
    summed = summed.reshape(row_span, col_span, block_size, block_size)
    return summed.transpose(0, 2, 1, 3).reshape(row_span * block_size, col_span * block_size)


def per_device(left_blocks, left_index, right_blocks, right_index):
    capacity = right_blocks.shape[1]
    owned_rows = PANEL // lax.axis_size("row")
    running_sum = jnp.zeros((BR * BS, BC * BS), jnp.float32)
    for section in range(STEPS):
        left_part, left_where = (
            lax.all_gather(left_blocks[section, 0], "col", axis=0, tiled=True),
            lax.all_gather(left_index[section, :, 0], "col", axis=1, tiled=True),
        )
        right_part, right_where = (
            lax.all_gather(right_blocks[section, :, 0], "row", axis=0, tiled=True),
            lax.all_gather(right_index[section, :, :, 0], "row", axis=1, tiled=True),
        )
        running_sum = running_sum + panel_product(
            left_part, left_where, right_part, right_where, capacity, owned_rows, BR, BC
        )
    return running_sum


def solution(mesh):
    placed = (
        P(None, "row", "col", None, None),
        P(None, None, "row", "col"),
        P(None, "row", "col", None, None),
        P(None, None, "row", "col"),
    )
    return jax.shard_map(
        per_device, mesh=mesh, in_specs=placed, out_specs=P("row", "col"), check_vma=False
    )
```

profile of v0, /device:TPU:6, one launch (start us, length us, event | category | flops | bytes accessed | tf_op | source)
XLA Modules:
  0.0 302.3 jit_solution(16109247648297327046)
XLA Ops:
  6.5 1.5 fusion.31
  8.1 1.7 slice_bitcast_fusion.1
  9.9 0.7 all-gather.13.cloned.1.call-update
  10.6 0.5 all-gather.15.cloned.1.call-update
  11.1 0.7 fusion.32
  11.9 0.7 fusion.33
  12.6 23.6 %all-gather.5 = s32[1,2,32,1]{1,3,0,2:T(1,128)S(1)} all-gather(s32[1,2,1,1]{1,3,0,2:T(1,128)S(1)} %get-tuple-element.20), channel_id=7, replica_groups=mesh['row'=32,'col'=16] {'row'}, dimensions={2}, use_global_device_ids=true | all-gather | bytes 264 | tf_op jit(solution)/shard_map/all_gather | solution.py:50
  36.2 32.6 %all-gather.4 = s32[1,2,1,32]{1,2,0,3:T(1,128)S(1)} all-gather(s32[1,2,1,2]{1,2,0,3:T(1,128)S(1)} %copy.39), channel_id=6, replica_groups=mesh['row'=32,'col'=16] {'col'}, dimensions={3}, use_global_device_ids=true | all-gather | bytes 272 | tf_op jit(solution)/shard_map/all_gather | solution.py:46
  68.8 1.3 multiply_reduce_fusion
  70.1 1.3 slice_reduce_fusion
  71.4 0.7 gather_fusion.4
  72.1 0.7 gather_fusion.3
  72.9 19.6 %all-gather.1 = s32[1,2,32,1]{1,3,0,2:T(1,128)S(1)} all-gather(s32[1,2,1,1]{1,3,0,2:T(1,128)S(1)} %get-tuple-element.19), channel_id=3, replica_groups=mesh['row'=32,'col'=16] {'row'}, dimensions={2}, use_global_device_ids=true | all-gather | bytes 264 | tf_op jit(solution)/shard_map/all_gather | solution.py:50
  92.5 25.9 %all-gather = s32[1,2,1,32]{1,2,0,3:T(1,128)S(1)} all-gather(s32[1,2,1,2]{1,2,0,3:T(1,128)S(1)} %copy.37), channel_id=2, replica_groups=mesh['row'=32,'col'=16] {'col'}, dimensions={3}, use_global_device_ids=true | all-gather | bytes 272 | tf_op jit(solution)/shard_map/all_gather | solution.py:46
  118.5 1.3 multiply_reduce_fusion.1
  119.8 1.3 slice_reduce_fusion.3
  121.0 0.7 gather_fusion.1
  121.7 0.7 gather_fusion
  122.5 0.7 compare_reduce_fusion
  123.1 0.7 compare_reduce_fusion.1
  123.9 2.3 gather_fusion.5
  126.2 22.7 %all-gather.19.cloned.1.call-done = f32[1,1,32,128,128]{4,3,1,0,2:T(8,128)} async-done(((f32[1,1,2,128,128]{4,3,1,0,2:T(8,128)}), f32[1,1,32,128,128]{4,3,1,0,2:T(8,128)}) %all-gather.19.cloned.1.call-update) | async-done | bytes 2097168 | tf_op jit(solution)/shard_map/all_gather | solution.py:45
  148.8 6.4 %fusion.11 = f32[32,128,128]{1,2,0:T(8,128)} fusion(f32[32,128,128]{2,1,0:T(8,128)S(1)} %gather_fusion.5, f32[1,1,32,128,128]{4,3,1,0,2:T(8,128)} %all-gather.19.cloned.1.call-done), kind=kOutput, calls=%fused_computation.15 | convolution fusion | flops 805306368 | bytes 6291456 | tf_op jit(solution)/shard_map/lab,lqbc->lqac/dot_general | solution.py:27
  155.3 3.1 %copy.32 = f32[32,128,128]{2,0,1:T(8,128)} copy(f32[32,128,128]{1,2,0:T(8,128)} %fusion.11) | data formatting | bytes 4194304 | tf_op jit(solution)/shard_map/reshape.17
  158.4 49.0 %all-gather.13.cloned.1.call-done = f32[32,1,1,128,128]{4,3,2,1,0:T(8,128)} async-done(((f32[1,1,1,128,128]{4,3,2,1,0:T(8,128)}), f32[32,1,1,128,128]{4,3,2,1,0:T(8,128)}) %all-gather.13.cloned.1.call-update) | async-done | bytes 2097168 | tf_op jit(solution)/shard_map/all_gather | solution.py:49
  207.4 2.3 gather_fusion.2
  209.7 72.6 %all-gather.15.cloned.1.call-done = f32[1,1,32,128,128]{4,3,1,0,2:T(8,128)} async-done(((f32[1,1,2,128,128]{4,3,1,0,2:T(8,128)}), f32[1,1,32,128,128]{4,3,1,0,2:T(8,128)}) %all-gather.15.cloned.1.call-update) | async-done | bytes 2097168 | tf_op jit(solution)/shard_map/all_gather | solution.py:45
  282.2 6.4 %fusion.8 = f32[32,128,128]{1,2,0:T(8,128)} fusion(f32[32,128,128]{2,1,0:T(8,128)S(1)} %gather_fusion.2, f32[1,1,32,128,128]{4,3,1,0,2:T(8,128)} %all-gather.15.cloned.1.call-done), kind=kOutput, calls=%fused_computation.14 | convolution fusion | flops 805306368 | bytes 6291456 | tf_op jit(solution)/shard_map/lab,lqbc->lqac/dot_general | solution.py:27
  288.6 3.3 %copy.27 = f32[32,128,128]{2,0,1:T(8,128)} copy(f32[32,128,128]{1,2,0:T(8,128)} %fusion.8) | data formatting | bytes 4194304 | tf_op jit(solution)/shard_map/reshape.10
  291.9 1.2 fusion
  293.4 1.3 fusion.14
  294.8 1.0 copy.43
  (22 shorter events, 0.8 us)
Async XLA Ops:
  6.5 117.3 %all-gather.17.cloned.1.call-start = ((), (), s32[]{:S(2)}) async-start(), calls=%async_computation.2 | async-start | bytes 2162688 | tf_op jit(solution)/shard_map/all_gather | solution.py:49
  8.1 140.8 %all-gather.19.cloned.1.call-start = ((), (), s32[]{:S(2)}) async-start(), calls=%async_computation.3 | async-start | bytes 2228224 | tf_op jit(solution)/shard_map/all_gather | solution.py:45
  9.8 197.5 %all-gather.13.cloned.1.call-start = ((), (), s32[]{:S(2)}) async-start(), calls=%async_computation | async-start | bytes 2162688 | tf_op jit(solution)/shard_map/all_gather | solution.py:49
  10.6 271.7 %all-gather.15.cloned.1.call-start = ((), (), s32[]{:S(2)}) async-start(), calls=%async_computation.1 | async-start | bytes 2228224 | tf_op jit(solution)/shard_map/all_gather | solution.py:45
  288.6 3.3 %copy-start = (f32[32,128,128]{2,0,1:T(8,128)S(1)}, f32[32,128,128]{2,0,1:T(8,128)}, u32[]{:S(2)}) copy-start(f32[32,128,128]{2,0,1:T(8,128)} %copy.32) | copy-start | bytes 6291460
  291.9 1.6 copy-start.1
Sparse Core Ops, SparseCore 0:
  10.5 63.0 all-gather.16
  75.7 73.1 all-gather.18
  152.0 55.3 all-gather.12
  209.3 72.8 all-gather.14
where the time goes:
time: 303 us; the launch traced here: 302 us
  waiting for transfers between devices  145 us (48%)
  blocking collectives  102 us (34%)
  local copies, waits for them, and re-layouts  22.5 us (7%)
  matrix products  15.2 us (5%)
  between operations  13.2 us (4%)
  other arithmetic  3.92 us (1%)
    all_gather x2, waiting for transfers between devices, per_device(): lax.all_gather(left_blocks[section, 0], 'col', axis=0, tiled=True)  95.3 us
    all_gather x2, blocking collectives, per_device(): lax.all_gather(left_index[section, :, 0], 'col', axis=1, tiled=True)  58.5 us
    all_gather x2, waiting for transfers between devices, per_device(): lax.all_gather(right_blocks[section, :, 0], 'row', axis=0, tiled=True)  49 us
    all_gather x2, blocking collectives, per_device(): lax.all_gather(right_index[section, :, :, 0], 'row', axis=1, tiled=True)  43.3 us
    dot_general x2, matrix products, panel_product(): jnp.einsum('lab,lqbc->lqac', left_part, right_pick, precision=precise_mode)  12.8 us
    another operation x2, local copies, waits for them, and re-layouts  6.41 us
  transfers between devices with their start and end apart: 4, of which 3 were waited for; matrix products, arithmetic and copies ran while one was open for 9% of the time, Pallas kernels for 0%

commit v1 on v0

v1 whole, which is shorter than its diff:
```python
import jax
import jax.numpy as jnp
from jax import lax
from jax.experimental import pallas as pl
from jax.experimental.pallas import tpu as pltpu
from jax.sharding import PartitionSpec as P

BS = 128
STEPS = 2
BR = 4
BC = 4
LCAP = 2
N_ROW = 32
N_COL = 16
SLOTS = STEPS * LCAP
UNROLL = 4
F32 = jnp.float32


def along_col(x, step):
    return lax.ppermute(x, "col", [(z, (z + step) % N_COL) for z in range(N_COL)])


def packed(blocks, index):
    where = index.reshape(1, -1).astype(F32)
    where = jnp.pad(where, ((0, 7), (0, BS - where.shape[1])))
    return jnp.concatenate([blocks.reshape(-1, BS), where], axis=0)


def split(x):
    high = x.astype(jnp.bfloat16)
    return high, (x - high.astype(F32)).astype(jnp.bfloat16)


def product_kernel(right, *refs):
    lefts, out_ref = refs[:N_COL], refs[N_COL]
    l_buf, r_buf, l_where, r_where, todo, acc, where_sem, sem = refs[N_COL + 1 :]
    tile = pl.ds(SLOTS * BS, 8)
    wheres = [pltpu.make_async_copy(right.at[:, pl.ds(STEPS * BS, 8)], r_where, where_sem.at[N_COL])]
    blocks = [pltpu.make_async_copy(right, r_buf, sem.at[N_COL])]
    for u, left in enumerate(lefts):
        wheres.append(pltpu.make_async_copy(left.at[tile], l_where.at[u], where_sem.at[u]))
        blocks.append(pltpu.make_async_copy(left, l_buf.at[u], sem.at[u]))
    for copy in wheres + blocks:
        copy.start()
    acc[...] = jnp.zeros_like(acc)
    for copy in wheres:
        copy.wait()

    def look(u, count):
        for s in range(STEPS):
            for t in range(LCAP):
                i = l_where[u, 0, s * 2 * LCAP + t].astype(jnp.int32)
                k = l_where[u, 0, s * 2 * LCAP + LCAP + t].astype(jnp.int32)
                k = jnp.clip(k, 0, N_ROW - 1)
                row = r_where[k, 0, s * 2].astype(jnp.int32)
                j = r_where[k, 0, s * 2 + 1].astype(jnp.int32)
                todo[0, count] = u
                todo[1, count] = (s * LCAP + t) * BS
                todo[2, count] = k
                todo[3, count] = s * BS
                todo[4, count] = i * BC + j
                count = count + ((i >= 0) & (row == k)).astype(jnp.int32)
        return count

    count = lax.fori_loop(0, N_COL, look, jnp.int32(0))
    for n in range(UNROLL - 1):
        for field in range(4):
            todo[field, count + n] = 0
        todo[4, count + n] = BR * BC
    for copy in blocks:
        copy.wait()

    def multiply(step, carry):
        sums = []
        for n in range(UNROLL):
            at = step * UNROLL + n
            a = l_buf[todo[0, at], pl.ds(pl.multiple_of(todo[1, at], BS), BS), :]
            b = r_buf[todo[2, at], pl.ds(pl.multiple_of(todo[3, at], BS), BS), :]
            a = jnp.concatenate(split(a), axis=1)
            b = jnp.concatenate(split(b), axis=1)
            both = jnp.dot(a, jnp.concatenate([b, b], axis=0), preferred_element_type=F32)
            sums.append(both[:, :BS] + both[:, BS:])
        for n in range(UNROLL):
            acc[todo[4, step * UNROLL + n]] += sums[n]
        return carry

    lax.fori_loop(0, (count + UNROLL - 1) // UNROLL, multiply, 0)
    for i in range(BR):
        for j in range(BC):
            out_ref[pl.ds(i * BS, BS), pl.ds(j * BS, BS)] = acc[i * BC + j]


def products(lefts, right):
    most = N_COL * SLOTS + UNROLL
    hbm = pl.BlockSpec(memory_space=pltpu.HBM)
    return pl.pallas_call(
        product_kernel,
        out_shape=jax.ShapeDtypeStruct((BR * BS, BC * BS), F32),
        in_specs=[hbm] * (N_COL + 1),
        out_specs=pl.BlockSpec(memory_space=pltpu.VMEM),
        scratch_shapes=[
            pltpu.VMEM((N_COL,) + lefts[0].shape, F32),
            pltpu.VMEM(right.shape, F32),
            pltpu.SMEM((N_COL, 8, BS), F32),
            pltpu.SMEM((N_ROW, 8, BS), F32),
            pltpu.SMEM((5, most), jnp.int32),
            pltpu.VMEM((BR * BC + 1, BS, BS), F32),
            pltpu.SemaphoreType.DMA((N_COL + 1,)),
            pltpu.SemaphoreType.DMA((N_COL + 1,)),
        ],
        compiler_params=pltpu.CompilerParams(vmem_limit_bytes=48 * 1024 * 1024),
    )(right, *lefts)


def per_device(left_blocks, left_index, right_blocks, right_index):
    own = packed(left_blocks, left_index)
    right = lax.all_gather(packed(right_blocks, right_index), "row", axis=0)
    lefts, up, down = [own], own, own
    for hop in range(1, N_COL // 2 + 1):
        up = along_col(up, 1)
        lefts.append(up)
        if hop < N_COL // 2:
            down = along_col(down, -1)
            lefts.append(down)
    return products(lefts, right)


def solution(mesh):
    placed = (
        P(None, "row", "col", None, None),
        P(None, None, "row", "col"),
        P(None, "row", "col", None, None),
        P(None, None, "row", "col"),
    )
    return jax.shard_map(
        per_device, mesh=mesh, in_specs=placed, out_specs=P("row", "col"), check_vma=False
    )
```

time: 303 us -> 117 us (0.39)
  waiting for transfers between devices: 145 us -> 27.7 us
  blocking collectives: 102 us -> 0 us
  starting transfers between devices: 0.12 us -> 57.5 us
  local copies, waits for them, and re-layouts: 22.5 us -> 5.14 us
  matrix products: 15.2 us -> 0 us
  Pallas kernels: 0 us -> 7.24 us
    all_gather x4 -> x1, waiting for transfers between devices: 144 us -> 0.01 us  [per_device(): right = lax.all_gather(packed(right_blocks, right_index), 'row', axis=0)]
    all_gather x4 -> x0, blocking collectives: 102 us -> none  [the longest x2 58.5 us: per_device(): lax.all_gather(left_index[section, :, 0], 'col', axis=1, tiled=True)]
    ppermute x0 -> x15, starting transfers between devices: none -> 57.5 us  [along_col(): lax.ppermute(x, 'col', [(z, (z + step) % N_COL) for z in range(N_COL)])]
    ppermute x0 -> x15, waiting for transfers between devices: none -> 27.7 us  [along_col(): lax.ppermute(x, 'col', [(z, (z + step) % N_COL) for z in range(N_COL)])]
    dot_general x4 -> x0, matrix products: 15.2 us -> none  [the longest x2 12.8 us: panel_product(): jnp.einsum('lab,lqbc->lqac', left_part, right_pick, precision=precise_mode)]
    gather x6 -> x0, local copies, waits for them, and re-layouts: 7.37 us -> none  [the longest x2 4.56 us: panel_product(): right_pick = right_part[picked]]
    pallas_call x0 -> x1, Pallas kernels: none -> 7.24 us  [products(): pl.pallas_call(product_kernel, out_shape=jax.ShapeDtypeStruct((BR * BS, B...]
    another operation x2 -> x0, local copies, waits for them, and re-layouts: 6.41 us -> none
  transfers between devices with their start and end apart: 4 -> 16, of which waited for: 3 -> 8; matrix products, arithmetic and copies ran while one was open for 9% -> 2% of each run, Pallas kernels for 0% -> 0%
where the time goes in v1:
time: 117 us; the launch traced here: 115 us
  starting transfers between devices  57.5 us (49%)
  waiting for transfers between devices  27.7 us (24%)
  between operations  13.6 us (12%)
  Pallas kernels  7.24 us (6%)
  local copies, waits for them, and re-layouts  5.14 us (4%)
  other arithmetic  3.96 us (3%)
    ppermute x15, starting transfers between devices, along_col(): lax.ppermute(x, 'col', [(z, (z + step) % N_COL) for z in range(N_COL)])  57.5 us
    ppermute x15, waiting for transfers between devices, along_col(): lax.ppermute(x, 'col', [(z, (z + step) % N_COL) for z in range(N_COL)])  27.7 us
    pallas_call x1, Pallas kernels, products(): pl.pallas_call(product_kernel, out_shape=jax.ShapeDtypeStruct((BR * BS, B...  7.24 us
    unnamed x12, local copies, waits for them, and re-layouts  4.97 us
    concatenate x2, other arithmetic, packed(): return jnp.concatenate([blocks.reshape(-1, BS), where], axis=0)  2.56 us
  transfers between devices with their start and end apart: 16, of which 8 were waited for; matrix products, arithmetic and copies ran while one was open for 2% of the time, Pallas kernels for 0%

profile of v1, /device:TPU:6, one launch (start us, length us, event | category | flops | bytes accessed | tf_op | source)
XLA Modules:
  0.0 115.1 jit_solution(6168324065266239302)
XLA Ops:
  7.3 1.6 %select_maximum_fusion.1 = f32[264,128]{1,0:T(8,128)} fusion(f32[1,4]{1,0:T(1,128)S(1)} %convert_element_type.33, f32[256,128]{1,0:T(8,128)} %bitcast.5), kind=kLoop, calls=%fused_computation.2 | loop fusion | flops 101376 | bytes 266256 | tf_op jit(solution)/shard_map/concatenate | solution.py:27
  8.9 0.7 convert_reduce_fusion
  9.7 1.0 select_maximum_fusion.refs_0_
  10.7 3.8 %collective-permute-start = (f32[520,128]{1,0:T(8,128)S(1)}, f32[520,128]{1,0:T(8,128)S(1)}, u32[]{:S(2)}, u32[]{:S(2)}) collective-permute-start(f32[520,128]{1,0:T(8,128)S(1)} %select_maximum_fusion.refs_0_), channel_id=1, source_target_pairs={{0,1},{1,2},{2,3},{3,4},{4,5},{5,6},{6,7},{7,8},{8,9},{9,10},{10,1... | collective-permute-start | bytes 798728 | tf_op jit(solution)/shard_map/ppermute | solution.py:21
  14.5 9.5 %collective-permute-start.1 = (f32[520,128]{1,0:T(8,128)S(1)}, f32[520,128]{1,0:T(8,128)S(1)}, u32[]{:S(2)}, u32[]{:S(2)}) collective-permute-start(f32[520,128]{1,0:T(8,128)S(1)} %select_maximum_fusion.refs_0_), channel_id=1, source_target_pairs={{0,15},{1,0},{2,1},{3,2},{4,3},{5,4},{6,5},{7,6},{8,7},{9,8},{10,9... | collective-permute-start | bytes 798728 | tf_op jit(solution)/shard_map/ppermute | solution.py:21
  24.0 4.4 %collective-permute-done.refs_1_ = f32[520,128]{1,0:T(8,128)S(1)} collective-permute-done((f32[520,128]{1,0:T(8,128)S(1)}, f32[520,128]{1,0:T(8,128)S(1)}, u32[]{:S(2)}, u32[]{:S(2)}) %collective-permute-start) | collective-permute-done | bytes 266272 | tf_op jit(solution)/shard_map/ppermute | solution.py:21
  28.5 1.9 %collective-permute-start.2 = (f32[520,128]{1,0:T(8,128)S(1)}, f32[520,128]{1,0:T(8,128)S(1)}, u32[]{:S(2)}, u32[]{:S(2)}) collective-permute-start(f32[520,128]{1,0:T(8,128)S(1)} %collective-permute-done.refs_1_), channel_id=1, source_target_pairs={{0,1},{1,2},{2,3},{3,4},{4,5},{5,6},{6,7},{7,8},{8,9},{9,10},{10,1... | collective-permute-start | bytes 798728 | tf_op jit(solution)/shard_map/ppermute | solution.py:21
  30.4 5.1 %collective-permute-start.3 = (f32[520,128]{1,0:T(8,128)S(1)}, f32[520,128]{1,0:T(8,128)S(1)}, u32[]{:S(2)}, u32[]{:S(2)}) collective-permute-start(f32[520,128]{1,0:T(8,128)S(1)} %collective-permute-done.1.refs_2_), channel_id=1, source_target_pairs={{0,15},{1,0},{2,1},{3,2},{4,3},{5,4},{6,5},{7,6},{8,7},{9,8},{10,9... | collective-permute-start | bytes 798728 | tf_op jit(solution)/shard_map/ppermute | solution.py:21
  35.6 3.6 %collective-permute-done.2.refs_3_ = f32[520,128]{1,0:T(8,128)S(1)} collective-permute-done((f32[520,128]{1,0:T(8,128)S(1)}, f32[520,128]{1,0:T(8,128)S(1)}, u32[]{:S(2)}, u32[]{:S(2)}) %collective-permute-start.2) | collective-permute-done | bytes 266272 | tf_op jit(solution)/shard_map/ppermute | solution.py:21
  39.2 1.9 %collective-permute-start.4 = (f32[520,128]{1,0:T(8,128)S(1)}, f32[520,128]{1,0:T(8,128)S(1)}, u32[]{:S(2)}, u32[]{:S(2)}) collective-permute-start(f32[520,128]{1,0:T(8,128)S(1)} %collective-permute-done.2.refs_3_), channel_id=1, source_target_pairs={{0,1},{1,2},{2,3},{3,4},{4,5},{5,6},{6,7},{7,8},{8,9},{9,10},{10,1... | collective-permute-start | bytes 798728 | tf_op jit(solution)/shard_map/ppermute | solution.py:21
  41.1 5.1 %collective-permute-start.5 = (f32[520,128]{1,0:T(8,128)S(1)}, f32[520,128]{1,0:T(8,128)S(1)}, u32[]{:S(2)}, u32[]{:S(2)}) collective-permute-start(f32[520,128]{1,0:T(8,128)S(1)} %collective-permute-done.3.refs_4_), channel_id=1, source_target_pairs={{0,15},{1,0},{2,1},{3,2},{4,3},{5,4},{6,5},{7,6},{8,7},{9,8},{10,9... | collective-permute-start | bytes 798728 | tf_op jit(solution)/shard_map/ppermute | solution.py:21
  46.2 2.8 %collective-permute-done.4.refs_5_ = f32[520,128]{1,0:T(8,128)S(1)} collective-permute-done((f32[520,128]{1,0:T(8,128)S(1)}, f32[520,128]{1,0:T(8,128)S(1)}, u32[]{:S(2)}, u32[]{:S(2)}) %collective-permute-start.4) | collective-permute-done | bytes 266272 | tf_op jit(solution)/shard_map/ppermute | solution.py:21
  49.0 1.9 %collective-permute-start.6 = (f32[520,128]{1,0:T(8,128)S(1)}, f32[520,128]{1,0:T(8,128)S(1)}, u32[]{:S(2)}, u32[]{:S(2)}) collective-permute-start(f32[520,128]{1,0:T(8,128)S(1)} %collective-permute-done.4.refs_5_), channel_id=1, source_target_pairs={{0,1},{1,2},{2,3},{3,4},{4,5},{5,6},{6,7},{7,8},{8,9},{9,10},{10,1... | collective-permute-start | bytes 798728 | tf_op jit(solution)/shard_map/ppermute | solution.py:21
  50.9 5.1 %collective-permute-start.7 = (f32[520,128]{1,0:T(8,128)S(1)}, f32[520,128]{1,0:T(8,128)S(1)}, u32[]{:S(2)}, u32[]{:S(2)}) collective-permute-start(f32[520,128]{1,0:T(8,128)S(1)} %collective-permute-done.5.refs_6_), channel_id=1, source_target_pairs={{0,15},{1,0},{2,1},{3,2},{4,3},{5,4},{6,5},{7,6},{8,7},{9,8},{10,9... | collective-permute-start | bytes 798728 | tf_op jit(solution)/shard_map/ppermute | solution.py:21
  56.1 2.4 %collective-permute-done.6.refs_7_ = f32[520,128]{1,0:T(8,128)S(1)} collective-permute-done((f32[520,128]{1,0:T(8,128)S(1)}, f32[520,128]{1,0:T(8,128)S(1)}, u32[]{:S(2)}, u32[]{:S(2)}) %collective-permute-start.6) | collective-permute-done | bytes 266272 | tf_op jit(solution)/shard_map/ppermute | solution.py:21
  58.5 1.9 %collective-permute-start.8 = (f32[520,128]{1,0:T(8,128)S(1)}, f32[520,128]{1,0:T(8,128)S(1)}, u32[]{:S(2)}, u32[]{:S(2)}) collective-permute-start(f32[520,128]{1,0:T(8,128)S(1)} %collective-permute-done.6.refs_7_), channel_id=1, source_target_pairs={{0,1},{1,2},{2,3},{3,4},{4,5},{5,6},{6,7},{7,8},{8,9},{9,10},{10,1... | collective-permute-start | bytes 798728 | tf_op jit(solution)/shard_map/ppermute | solution.py:21
  60.5 5.1 %collective-permute-start.9 = (f32[520,128]{1,0:T(8,128)S(1)}, f32[520,128]{1,0:T(8,128)S(1)}, u32[]{:S(2)}, u32[]{:S(2)}) collective-permute-start(f32[520,128]{1,0:T(8,128)S(1)} %collective-permute-done.7.refs_8_), channel_id=1, source_target_pairs={{0,15},{1,0},{2,1},{3,2},{4,3},{5,4},{6,5},{7,6},{8,7},{9,8},{10,9... | collective-permute-start | bytes 798728 | tf_op jit(solution)/shard_map/ppermute | solution.py:21
  65.6 2.4 %collective-permute-done.8.refs_9_ = f32[520,128]{1,0:T(8,128)S(1)} collective-permute-done((f32[520,128]{1,0:T(8,128)S(1)}, f32[520,128]{1,0:T(8,128)S(1)}, u32[]{:S(2)}, u32[]{:S(2)}) %collective-permute-start.8) | collective-permute-done | bytes 266272 | tf_op jit(solution)/shard_map/ppermute | solution.py:21
  68.0 1.9 %collective-permute-start.10 = (f32[520,128]{1,0:T(8,128)S(1)}, f32[520,128]{1,0:T(8,128)S(1)}, u32[]{:S(2)}, u32[]{:S(2)}) collective-permute-start(f32[520,128]{1,0:T(8,128)S(1)} %collective-permute-done.8.refs_9_), channel_id=1, source_target_pairs={{0,1},{1,2},{2,3},{3,4},{4,5},{5,6},{6,7},{7,8},{8,9},{9,10},{10,1... | collective-permute-start | bytes 798728 | tf_op jit(solution)/shard_map/ppermute | solution.py:21
  70.0 5.1 %collective-permute-start.11 = (f32[520,128]{1,0:T(8,128)S(1)}, f32[520,128]{1,0:T(8,128)S(1)}, u32[]{:S(2)}, u32[]{:S(2)}) collective-permute-start(f32[520,128]{1,0:T(8,128)S(1)} %collective-permute-done.9.refs_10_), channel_id=1, source_target_pairs={{0,15},{1,0},{2,1},{3,2},{4,3},{5,4},{6,5},{7,6},{8,7},{9,8},{10,9... | collective-permute-start | bytes 798728 | tf_op jit(solution)/shard_map/ppermute | solution.py:21
  75.1 2.4 %collective-permute-done.10.refs_11_ = f32[520,128]{1,0:T(8,128)S(1)} collective-permute-done((f32[520,128]{1,0:T(8,128)S(1)}, f32[520,128]{1,0:T(8,128)S(1)}, u32[]{:S(2)}, u32[]{:S(2)}) %collective-permute-start.10) | collective-permute-done | bytes 266272 | tf_op jit(solution)/shard_map/ppermute | solution.py:21
  77.5 1.9 %collective-permute-start.12 = (f32[520,128]{1,0:T(8,128)S(1)}, f32[520,128]{1,0:T(8,128)S(1)}, u32[]{:S(2)}, u32[]{:S(2)}) collective-permute-start(f32[520,128]{1,0:T(8,128)S(1)} %collective-permute-done.10.refs_11_), channel_id=1, source_target_pairs={{0,1},{1,2},{2,3},{3,4},{4,5},{5,6},{6,7},{7,8},{8,9},{9,10},{10,1... | collective-permute-start | bytes 798728 | tf_op jit(solution)/shard_map/ppermute | solution.py:21
  79.5 5.1 %collective-permute-start.13 = (f32[520,128]{1,0:T(8,128)S(1)}, f32[520,128]{1,0:T(8,128)S(1)}, u32[]{:S(2)}, u32[]{:S(2)}) collective-permute-start(f32[520,128]{1,0:T(8,128)S(1)} %collective-permute-done.11.refs_12_), channel_id=1, source_target_pairs={{0,15},{1,0},{2,1},{3,2},{4,3},{5,4},{6,5},{7,6},{8,7},{9,8},{10,9... | collective-permute-start | bytes 798728 | tf_op jit(solution)/shard_map/ppermute | solution.py:21
  84.6 3.3 %collective-permute-done.12.refs_13_ = f32[520,128]{1,0:T(8,128)S(1)} collective-permute-done((f32[520,128]{1,0:T(8,128)S(1)}, f32[520,128]{1,0:T(8,128)S(1)}, u32[]{:S(2)}, u32[]{:S(2)}) %collective-permute-start.12) | collective-permute-done | bytes 266272 | tf_op jit(solution)/shard_map/ppermute | solution.py:21
  88.0 1.9 %collective-permute-start.14 = (f32[520,128]{1,0:T(8,128)S(1)}, f32[520,128]{1,0:T(8,128)S(1)}, u32[]{:S(2)}, u32[]{:S(2)}) collective-permute-start(f32[520,128]{1,0:T(8,128)S(1)} %collective-permute-done.12.refs_13_), channel_id=1, source_target_pairs={{0,1},{1,2},{2,3},{3,4},{4,5},{5,6},{6,7},{7,8},{8,9},{9,10},{10,1... | collective-permute-start | bytes 798728 | tf_op jit(solution)/shard_map/ppermute | solution.py:21
  90.6 0.7 copy-done.2
  91.3 6.2 %collective-permute-done.14.refs_15_ = f32[520,128]{1,0:T(8,128)S(1)} collective-permute-done((f32[520,128]{1,0:T(8,128)S(1)}, f32[520,128]{1,0:T(8,128)S(1)}, u32[]{:S(2)}, u32[]{:S(2)}) %collective-permute-start.14) | collective-permute-done | bytes 266272 | tf_op jit(solution)/shard_map/ppermute | solution.py:21
  97.5 0.7 copy-done.4
  98.2 0.9 copy-done.1
  99.1 0.9 copy-done.3
  100.1 0.9 copy-done.5
  101.0 7.2 %shard_map.46 = f32[512,512]{1,0:T(8,128)} custom-call(f32[32,264,128]{2,1,0:T(8,128)} %bitcast.3, f32[520,128]{1,0:T(8,128)S(1)} %select_maximum_fusion.refs_0_, f32[520,128]{1,0:T(8,128)S(1)} %collective-permute-done.refs_1_, f32[520,128]{1,0:T(8,128)S(1)} %collective-permute-done.1.refs_2_, f32[520,128]{1,0:T(8,128)S(1)} %collective-permute-done.2.refs_3_, ...), custom_call_target="tpu_custom_call" | custom-call | tf_op jit(solution)/shard_map/pallas_call | solution.py:97
  (20 shorter events, 1.6 us)
Async XLA Ops:
  6.5 91.6 %all-gather.3.cloned.1.call-start = ((), (), s32[]{:S(2)}) async-start(), calls=%async_computation | async-start | bytes 4460544 | tf_op jit(solution)/shard_map/all_gather | solution.py:118
  10.7 17.8 %collective-permute-start = (f32[520,128]{1,0:T(8,128)S(1)}, f32[520,128]{1,0:T(8,128)S(1)}, u32[]{:S(2)}, u32[]{:S(2)}) collective-permute-start(f32[520,128]{1,0:T(8,128)S(1)} %select_maximum_fusion.refs_0_), channel_id=1, source_target_pairs={{0,1},{1,2},{2,3},{3,4},{4,5},{5,6},{6,7},{7,8},{8,9},{9,10},{10,1... | collective-permute-start | bytes 798728 | tf_op jit(solution)/shard_map/ppermute | solution.py:21
  14.5 15.9 %collective-permute-start.1 = (f32[520,128]{1,0:T(8,128)S(1)}, f32[520,128]{1,0:T(8,128)S(1)}, u32[]{:S(2)}, u32[]{:S(2)}) collective-permute-start(f32[520,128]{1,0:T(8,128)S(1)} %select_maximum_fusion.refs_0_), channel_id=1, source_target_pairs={{0,15},{1,0},{2,1},{3,2},{4,3},{5,4},{6,5},{7,6},{8,7},{9,8},{10,9... | collective-permute-start | bytes 798728 | tf_op jit(solution)/shard_map/ppermute | solution.py:21
  28.5 10.7 %collective-permute-start.2 = (f32[520,128]{1,0:T(8,128)S(1)}, f32[520,128]{1,0:T(8,128)S(1)}, u32[]{:S(2)}, u32[]{:S(2)}) collective-permute-start(f32[520,128]{1,0:T(8,128)S(1)} %collective-permute-done.refs_1_), channel_id=1, source_target_pairs={{0,1},{1,2},{2,3},{3,4},{4,5},{5,6},{6,7},{7,8},{8,9},{9,10},{10,1... | collective-permute-start | bytes 798728 | tf_op jit(solution)/shard_map/ppermute | solution.py:21
  30.4 10.7 %collective-permute-start.3 = (f32[520,128]{1,0:T(8,128)S(1)}, f32[520,128]{1,0:T(8,128)S(1)}, u32[]{:S(2)}, u32[]{:S(2)}) collective-permute-start(f32[520,128]{1,0:T(8,128)S(1)} %collective-permute-done.1.refs_2_), channel_id=1, source_target_pairs={{0,15},{1,0},{2,1},{3,2},{4,3},{5,4},{6,5},{7,6},{8,7},{9,8},{10,9... | collective-permute-start | bytes 798728 | tf_op jit(solution)/shard_map/ppermute | solution.py:21
  39.2 9.9 %collective-permute-start.4 = (f32[520,128]{1,0:T(8,128)S(1)}, f32[520,128]{1,0:T(8,128)S(1)}, u32[]{:S(2)}, u32[]{:S(2)}) collective-permute-start(f32[520,128]{1,0:T(8,128)S(1)} %collective-permute-done.2.refs_3_), channel_id=1, source_target_pairs={{0,1},{1,2},{2,3},{3,4},{4,5},{5,6},{6,7},{7,8},{8,9},{9,10},{10,1... | collective-permute-start | bytes 798728 | tf_op jit(solution)/shard_map/ppermute | solution.py:21
  41.1 9.8 %collective-permute-start.5 = (f32[520,128]{1,0:T(8,128)S(1)}, f32[520,128]{1,0:T(8,128)S(1)}, u32[]{:S(2)}, u32[]{:S(2)}) collective-permute-start(f32[520,128]{1,0:T(8,128)S(1)} %collective-permute-done.3.refs_4_), channel_id=1, source_target_pairs={{0,15},{1,0},{2,1},{3,2},{4,3},{5,4},{6,5},{7,6},{8,7},{9,8},{10,9... | collective-permute-start | bytes 798728 | tf_op jit(solution)/shard_map/ppermute | solution.py:21
  49.0 9.5 %collective-permute-start.6 = (f32[520,128]{1,0:T(8,128)S(1)}, f32[520,128]{1,0:T(8,128)S(1)}, u32[]{:S(2)}, u32[]{:S(2)}) collective-permute-start(f32[520,128]{1,0:T(8,128)S(1)} %collective-permute-done.4.refs_5_), channel_id=1, source_target_pairs={{0,1},{1,2},{2,3},{3,4},{4,5},{5,6},{6,7},{7,8},{8,9},{9,10},{10,1... | collective-permute-start | bytes 798728 | tf_op jit(solution)/shard_map/ppermute | solution.py:21
  50.9 9.5 %collective-permute-start.7 = (f32[520,128]{1,0:T(8,128)S(1)}, f32[520,128]{1,0:T(8,128)S(1)}, u32[]{:S(2)}, u32[]{:S(2)}) collective-permute-start(f32[520,128]{1,0:T(8,128)S(1)} %collective-permute-done.5.refs_6_), channel_id=1, source_target_pairs={{0,15},{1,0},{2,1},{3,2},{4,3},{5,4},{6,5},{7,6},{8,7},{9,8},{10,9... | collective-permute-start | bytes 798728 | tf_op jit(solution)/shard_map/ppermute | solution.py:21
  58.5 9.5 %collective-permute-start.8 = (f32[520,128]{1,0:T(8,128)S(1)}, f32[520,128]{1,0:T(8,128)S(1)}, u32[]{:S(2)}, u32[]{:S(2)}) collective-permute-start(f32[520,128]{1,0:T(8,128)S(1)} %collective-permute-done.6.refs_7_), channel_id=1, source_target_pairs={{0,1},{1,2},{2,3},{3,4},{4,5},{5,6},{6,7},{7,8},{8,9},{9,10},{10,1... | collective-permute-start | bytes 798728 | tf_op jit(solution)/shard_map/ppermute | solution.py:21
  60.5 9.5 %collective-permute-start.9 = (f32[520,128]{1,0:T(8,128)S(1)}, f32[520,128]{1,0:T(8,128)S(1)}, u32[]{:S(2)}, u32[]{:S(2)}) collective-permute-start(f32[520,128]{1,0:T(8,128)S(1)} %collective-permute-done.7.refs_8_), channel_id=1, source_target_pairs={{0,15},{1,0},{2,1},{3,2},{4,3},{5,4},{6,5},{7,6},{8,7},{9,8},{10,9... | collective-permute-start | bytes 798728 | tf_op jit(solution)/shard_map/ppermute | solution.py:21
  68.0 9.5 %collective-permute-start.10 = (f32[520,128]{1,0:T(8,128)S(1)}, f32[520,128]{1,0:T(8,128)S(1)}, u32[]{:S(2)}, u32[]{:S(2)}) collective-permute-start(f32[520,128]{1,0:T(8,128)S(1)} %collective-permute-done.8.refs_9_), channel_id=1, source_target_pairs={{0,1},{1,2},{2,3},{3,4},{4,5},{5,6},{6,7},{7,8},{8,9},{9,10},{10,1... | collective-permute-start | bytes 798728 | tf_op jit(solution)/shard_map/ppermute | solution.py:21
  70.0 9.5 %collective-permute-start.11 = (f32[520,128]{1,0:T(8,128)S(1)}, f32[520,128]{1,0:T(8,128)S(1)}, u32[]{:S(2)}, u32[]{:S(2)}) collective-permute-start(f32[520,128]{1,0:T(8,128)S(1)} %collective-permute-done.9.refs_10_), channel_id=1, source_target_pairs={{0,15},{1,0},{2,1},{3,2},{4,3},{5,4},{6,5},{7,6},{8,7},{9,8},{10,9... | collective-permute-start | bytes 798728 | tf_op jit(solution)/shard_map/ppermute | solution.py:21
  77.5 10.4 %collective-permute-start.12 = (f32[520,128]{1,0:T(8,128)S(1)}, f32[520,128]{1,0:T(8,128)S(1)}, u32[]{:S(2)}, u32[]{:S(2)}) collective-permute-start(f32[520,128]{1,0:T(8,128)S(1)} %collective-permute-done.10.refs_11_), channel_id=1, source_target_pairs={{0,1},{1,2},{2,3},{3,4},{4,5},{5,6},{6,7},{7,8},{8,9},{9,10},{10,1... | collective-permute-start | bytes 798728 | tf_op jit(solution)/shard_map/ppermute | solution.py:21
  79.5 11.1 %collective-permute-start.13 = (f32[520,128]{1,0:T(8,128)S(1)}, f32[520,128]{1,0:T(8,128)S(1)}, u32[]{:S(2)}, u32[]{:S(2)}) collective-permute-start(f32[520,128]{1,0:T(8,128)S(1)} %collective-permute-done.11.refs_12_), channel_id=1, source_target_pairs={{0,15},{1,0},{2,1},{3,2},{4,3},{5,4},{6,5},{7,6},{8,7},{9,8},{10,9... | collective-permute-start | bytes 798728 | tf_op jit(solution)/shard_map/ppermute | solution.py:21
  88.0 9.5 %collective-permute-start.14 = (f32[520,128]{1,0:T(8,128)S(1)}, f32[520,128]{1,0:T(8,128)S(1)}, u32[]{:S(2)}, u32[]{:S(2)}) collective-permute-start(f32[520,128]{1,0:T(8,128)S(1)} %collective-permute-done.12.refs_13_), channel_id=1, source_target_pairs={{0,1},{1,2},{2,3},{3,4},{4,5},{5,6},{6,7},{7,8},{8,9},{9,10},{10,1... | collective-permute-start | bytes 798728 | tf_op jit(solution)/shard_map/ppermute | solution.py:21
  89.9 0.7 copy-start
  90.6 0.7 copy-start.2
  97.5 0.7 copy-start.4
  98.2 1.0 copy-start.1
  99.1 1.0 copy-start.3
  100.1 1.0 copy-start.5
Sparse Core Ops, SparseCore 0:
  10.6 65.6 all-gather.2

commit v2 on v1

v2 whole, which is shorter than its diff:
```python
import jax
import jax.numpy as jnp
from jax import lax
from jax.experimental import pallas as pl
from jax.experimental.pallas import tpu as pltpu
from jax.sharding import PartitionSpec as P

BS = 128
STEPS = 2
BR = 4
BC = 4
LCAP = 2
N_ROW = 32
N_COL = 16
SIDE = 4
AREA = SIDE * SIDE
SLOTS = STEPS * LCAP
UNROLL = 4
PARTS = 4
MOST = N_COL * SLOTS
F32 = jnp.float32
I32 = jnp.int32


def along_row(x, dx, dy, dc):
    pairs = []
    for r in range(N_ROW):
        a, b, c = r // (2 * SIDE), r // 2 % SIDE, r % 2
        to = ((a + dx) % SIDE * SIDE + (b + dy) % SIDE) * 2 + (c ^ dc)
        pairs.append((r, to))
    return lax.ppermute(x, "row", pairs)


def packed(blocks, index):
    where = index.reshape(1, -1).astype(F32)
    where = jnp.pad(where, ((0, 7), (0, BS - where.shape[1])))
    return jnp.concatenate([blocks.reshape(-1, BS), where], axis=0)


def split(x):
    high = x.astype(jnp.bfloat16)
    return high, (x - high.astype(F32)).astype(jnp.bfloat16)


def match_kernel(me, l_where, mine, other, todo, r_where, sem):
    copies = [
        pltpu.make_async_copy(ref.at[:, pl.ds(STEPS * BS, 8)], r_where.at[h], sem.at[h])
        for h, ref in enumerate((mine, other))
    ]
    for copy in copies:
        copy.start()
    for copy in copies:
        copy.wait()

    def look(u, count):
        for s in range(STEPS):
            for t in range(LCAP):
                i = l_where[u * 2 * SLOTS + s * 2 * LCAP + t]
                k = jnp.clip(l_where[u * 2 * SLOTS + s * 2 * LCAP + LCAP + t], 0, N_ROW - 1)
                dx = (me[0] + SIDE - lax.shift_right_logical(k, 3)) & (SIDE - 1)
                dy = (me[1] + SIDE - (lax.shift_right_logical(k, 1) & (SIDE - 1))) & (SIDE - 1)
                half = (me[2] + k) & 1
                place = dy * SIDE + dx
                row = r_where[half, place, 0, s * 2].astype(I32)
                j = r_where[half, place, 0, s * 2 + 1].astype(I32)
                todo[0, count] = u
                todo[1, count] = (s * LCAP + t) * BS
                todo[2, count] = half * AREA + place
                todo[3, count] = s * BS
                todo[4, count] = i * BC + j
                count = count + ((i >= 0) & (row == k)).astype(I32)
        return count

    count = lax.fori_loop(0, N_COL, look, jnp.int32(0))
    for n in range(UNROLL - 1):
        for field in range(4):
            todo[field, count + n] = 0
        todo[4, count + n] = BR * BC
    todo[5, 0] = count


def product_kernel(todo, left, mine, other, out_ref, l_buf, r_buf, acc, l_sem, r_sem):
    count = todo[5, 0]
    rights = [
        pltpu.make_async_copy(ref, r_buf.at[pl.ds(h * AREA, AREA)], r_sem.at[h])
        for h, ref in enumerate((mine, other))
    ]
    lefts = [
        pltpu.make_async_copy(left.at[part], l_buf.at[part], l_sem.at[n])
        for n, part in enumerate(pl.ds(u, N_COL // PARTS) for u in range(0, N_COL, N_COL // PARTS))
    ]
    for copy in lefts + rights:
        copy.start()
    steps = lax.div(count + UNROLL - 1, UNROLL)
    acc[...] = jnp.zeros_like(acc)
    for copy in lefts + rights:
        copy.wait()

    def multiply(step, carry):
        sums = []
        for n in range(UNROLL):
            at = step * UNROLL + n
            a = l_buf[todo[0, at], pl.ds(pl.multiple_of(todo[1, at], BS), BS), :]
            b = r_buf[todo[2, at], pl.ds(pl.multiple_of(todo[3, at], BS), BS), :]
            a = jnp.concatenate(split(a), axis=1)
            b = jnp.concatenate(split(b), axis=1)
            both = jnp.dot(a, jnp.concatenate([b, b], axis=0), preferred_element_type=F32)
            sums.append(both[:, :BS] + both[:, BS:])
        for n in range(UNROLL):
            acc[todo[4, step * UNROLL + n]] += sums[n]
        return carry

    lax.fori_loop(0, steps, multiply, 0)
    for i in range(BR):
        for j in range(BC):
            out_ref[pl.ds(i * BS, BS), pl.ds(j * BS, BS)] = acc[i * BC + j]


HBM = pl.BlockSpec(memory_space=pltpu.HBM)
SMEM = pl.BlockSpec(memory_space=pltpu.SMEM)


def matches(me, l_where, mine, other):
    return pl.pallas_call(
        match_kernel,
        out_shape=jax.ShapeDtypeStruct((6, MOST + UNROLL), I32),
        in_specs=[SMEM, SMEM, HBM, HBM],
        out_specs=SMEM,
        scratch_shapes=[pltpu.SMEM((2, AREA, 8, BS), F32), pltpu.SemaphoreType.DMA((2,))],
        compiler_params=pltpu.CompilerParams(vmem_limit_bytes=60 * 1024 * 1024),
    )(me, l_where, mine, other)


def products(todo, left, mine, other):
    return pl.pallas_call(
        product_kernel,
        out_shape=jax.ShapeDtypeStruct((BR * BS, BC * BS), F32),
        in_specs=[SMEM, HBM, HBM, HBM],
        out_specs=pl.BlockSpec(memory_space=pltpu.VMEM),
        scratch_shapes=[
            pltpu.VMEM(left.shape, F32),
            pltpu.VMEM((2 * AREA,) + mine.shape[1:], F32),
            pltpu.VMEM((BR * BC + 1, BS, BS), F32),
            pltpu.SemaphoreType.DMA((PARTS,)),
            pltpu.SemaphoreType.DMA((2,)),
        ],
        compiler_params=pltpu.CompilerParams(vmem_limit_bytes=60 * 1024 * 1024),
    )(todo, left, mine, other)


def per_device(left_blocks, left_index, right_blocks, right_index):
    left = lax.all_gather(left_blocks.reshape(SLOTS * BS, BS), "col", axis=0)
    mine = packed(right_blocks, right_index)
    line = jnp.stack([mine, *[along_row(mine, d, 0, 0) for d in (1, 2, 3)]])
    l_index, line = lax.optimization_barrier((left_index, line))
    l_where = lax.all_gather(l_index.reshape(-1), "col", axis=0, tiled=True)
    area = jnp.concatenate([line, *[along_row(line, 0, d, 0) for d in (1, 2, 3)]])
    area, l_where = lax.optimization_barrier((area, l_where))
    other = along_row(area, 0, 0, 1)
    row = lax.axis_index("row")
    me = jnp.stack([row // (2 * SIDE), row // 2 % SIDE, row % 2]).astype(I32)
    todo = matches(me, l_where, area, other)
    return products(todo, left, area, other)


def solution(mesh):
    placed = (
        P(None, "row", "col", None, None),
        P(None, None, "row", "col"),
        P(None, "row", "col", None, None),
        P(None, None, "row", "col"),
    )
    return jax.shard_map(
        per_device, mesh=mesh, in_specs=placed, out_specs=P("row", "col"), check_vma=False
    )
```

time: 117 us -> 107 us (0.915)
  starting transfers between devices: 57.5 us -> 22.3 us
  blocking collectives: 0 us -> 27.6 us
  waiting for transfers between devices: 27.7 us -> 22.4 us
  Pallas kernels: 7.24 us -> 11.4 us
  local copies, waits for them, and re-layouts: 5.14 us -> 2.94 us
    ppermute x15 -> x7, starting transfers between devices: 57.5 us -> 22.3 us  [along_row(): return lax.ppermute(x, 'row', pairs)]
    optimization_barrier x0 -> x1, blocking collectives: none -> 27.6 us  [per_device(): area, l_where = lax.optimization_barrier((area, l_where))]
    ppermute x15 -> x7, waiting for transfers between devices: 27.7 us -> 9.07 us  [along_row(): return lax.ppermute(x, 'row', pairs)]
    all_gather x1, waiting for transfers between devices: 0.01 us -> 12.7 us  [per_device(): left = lax.all_gather(left_blocks.reshape(SLOTS * BS, BS), 'col', axis=0)]
    pallas_call x0 -> x1, Pallas kernels: none -> 5.27 us  [matches(): pl.pallas_call(match_kernel, out_shape=jax.ShapeDtypeStruct((6, MOST + UN...]
    unnamed x12 -> x7, local copies, waits for them, and re-layouts: 4.97 us -> 2.26 us
    another operation x0 -> x3, other arithmetic: none -> 1.54 us  [the longest x2 0.96 us: per_device(): line = jnp.stack([mine, *[along_row(mine, d, 0, 0) for d in (1, 2, 3)]])]
    optimization_barrier x0 -> x1, other arithmetic: none -> 1.35 us  [per_device(): l_index, line = lax.optimization_barrier((left_index, line))]
  transfers between devices with their start and end apart: 16 -> 8, of which waited for: 8 -> 4; matrix products, arithmetic and copies ran while one was open for 2% -> 7% of each run, Pallas kernels for 0% -> 5%
where the time goes in v2:
time: 107 us; the launch traced here: 106 us
  blocking collectives  27.6 us (26%)
  waiting for transfers between devices  22.4 us (21%)
  starting transfers between devices  22.3 us (21%)
  between operations  14.2 us (13%)
  Pallas kernels  11.4 us (11%)
  other arithmetic  4.94 us (5%)
  local copies, waits for them, and re-layouts  2.94 us (3%)
    optimization_barrier x1, blocking collectives, per_device(): area, l_where = lax.optimization_barrier((area, l_where))  27.6 us
    ppermute x7, starting transfers between devices, along_row(): return lax.ppermute(x, 'row', pairs)  22.3 us
    all_gather x1, waiting for transfers between devices, per_device(): left = lax.all_gather(left_blocks.reshape(SLOTS * BS, BS), 'col', axis=0)  12.7 us
    ppermute x7, waiting for transfers between devices, along_row(): return lax.ppermute(x, 'row', pairs)  9.07 us
    pallas_call x1, Pallas kernels, products(): pl.pallas_call(product_kernel, out_shape=jax.ShapeDtypeStruct((BR * BS, B...  6.14 us
    pallas_call x1, Pallas kernels, matches(): pl.pallas_call(match_kernel, out_shape=jax.ShapeDtypeStruct((6, MOST + UN...  5.27 us
    unnamed x7, local copies, waits for them, and re-layouts  2.26 us
  transfers between devices with their start and end apart: 8, of which 4 were waited for; matrix products, arithmetic and copies ran while one was open for 7% of the time, Pallas kernels for 5%

profile of v2, /device:TPU:6, one launch (start us, length us, event | category | flops | bytes accessed | tf_op | source)
XLA Modules:
  0.0 105.9 jit_solution(5112347211493428124)
XLA Ops:
  6.5 0.0 all-gather.2.cloned.1.call-start
  6.5 0.7 all-gather.2.cloned.1.call-update
  7.3 0.7 convert_reduce_fusion
  8.0 0.1 convert_element_type.17
  8.0 0.9 fusion
  9.0 3.3 %collective-permute-start.1 = (f32[264,128]{1,0:T(8,128)S(1)}, f32[264,128]{1,0:T(8,128)S(1)}, u32[]{:S(2)}, u32[]{:S(2)}) collective-permute-start(f32[264,128]{1,0:T(8,128)S(1)} %get-tuple-element.14), channel_id=1, source_target_pairs={{0,256},{16,272},{32,288},{48,304},{64,320},{80,336},{96,352},{112... | collective-permute-start | bytes 405512 | tf_op jit(solution)/shard_map/ppermute | solution.py:31
  12.3 6.4 %collective-permute-start = (f32[264,128]{1,0:T(8,128)S(1)}, f32[264,128]{1,0:T(8,128)S(1)}, u32[]{:S(2)}, u32[]{:S(2)}) collective-permute-start(f32[264,128]{1,0:T(8,128)S(1)} %get-tuple-element.14), channel_id=1, source_target_pairs={{0,128},{16,144},{32,160},{48,176},{64,192},{80,208},{96,224},{112... | collective-permute-start | bytes 405512 | tf_op jit(solution)/shard_map/ppermute | solution.py:31
  18.7 2.8 %collective-permute-start.2 = (f32[264,128]{1,0:T(8,128)S(1)}, f32[264,128]{1,0:T(8,128)S(1)}, u32[]{:S(2)}, u32[]{:S(2)}) collective-permute-start(f32[264,128]{1,0:T(8,128)S(1)} %get-tuple-element.14), channel_id=1, source_target_pairs={{0,384},{16,400},{32,416},{48,432},{64,448},{80,464},{96,480},{112... | collective-permute-start | bytes 405512 | tf_op jit(solution)/shard_map/ppermute | solution.py:31
  21.4 0.0 collective-permute-done.1
  21.4 1.0 collective-permute-done
  22.5 4.3 %collective-permute-done.2 = f32[264,128]{1,0:T(8,128)S(1)} collective-permute-done((f32[264,128]{1,0:T(8,128)S(1)}, f32[264,128]{1,0:T(8,128)S(1)}, u32[]{:S(2)}, u32[]{:S(2)}) %collective-permute-start.2) | collective-permute-done | bytes 135200 | tf_op jit(solution)/shard_map/ppermute | solution.py:31
  26.8 2.6 %collective-permute-start.5 = (f32[4,264,128]{2,1,0:T(8,128)S(1)}, f32[4,264,128]{2,1,0:T(8,128)S(1)}, u32[]{:S(2)}, u32[]{:S(2)}) collective-permute-start(f32[4,264,128]{2,1,0:T(8,128)S(1)} %pad_maximum_fusion.1), channel_id=1, source_target_pairs={{0,96},{16,112},{32,0},{48,16},{64,32},{80,48},{96,64},{112,80},{1... | collective-permute-start | bytes 1622024 | tf_op jit(solution)/shard_map/ppermute | solution.py:31
  29.4 2.5 %collective-permute-start.4 = (f32[4,264,128]{2,1,0:T(8,128)S(1)}, f32[4,264,128]{2,1,0:T(8,128)S(1)}, u32[]{:S(2)}, u32[]{:S(2)}) collective-permute-start(f32[4,264,128]{2,1,0:T(8,128)S(1)} %pad_maximum_fusion.1), channel_id=1, source_target_pairs={{0,64},{16,80},{32,96},{48,112},{64,0},{80,16},{96,32},{112,48},{1... | collective-permute-start | bytes 1622024 | tf_op jit(solution)/shard_map/ppermute | solution.py:31
  31.9 2.9 %collective-permute-start.3 = (f32[4,264,128]{2,1,0:T(8,128)S(1)}, f32[4,264,128]{2,1,0:T(8,128)}, u32[]{:S(2)}, u32[]{:S(2)}) collective-permute-start(f32[4,264,128]{2,1,0:T(8,128)S(1)} %pad_maximum_fusion.1), channel_id=1, source_target_pairs={{0,32},{16,48},{32,64},{48,80},{64,96},{80,112},{96,0},{112,16},{1... | collective-permute-start | bytes 1622024 | tf_op jit(solution)/shard_map/ppermute | solution.py:31
  34.8 1.3 %dynamic-slice = u32[1]{0:T(128)} dynamic-slice(u32[512]{0:T(512)} %constant.61, u32[]{:T(128)S(6)} %add.13), dynamic_slice_sizes={1} | dynamic-slice | bytes 12
  36.8 0.5 broadcast.21
  37.3 1.3 %reduce.7 = s32[2,2,2]{2,1,0:T(2,128)S(1)} reduce(s32[2,2,1,2]{3,2,1,0:T(1,128)} %param.5, s32[]{:T(128)} %broadcast.21), dimensions={2}, to_apply=%get-tuple-element.10.reduce_sub_computation.3 | reduce | bytes 68 | tf_op jit(solution)/shard_map/optimization_barrier | solution.py:155
  38.6 0.1 reshape.22
  38.7 0.2 dynamic-update-slice
  38.9 27.6 %all-reduce.1.l_where = s32[128]{0:T(128)} all-reduce(s32[128]{0:T(128)S(1)} %dynamic-update-slice), channel_id=1, replica_groups=mesh['row'=32,'col'=16] {'col'}, use_global_device_ids=true, to_apply=%add.1 | all-reduce | flops 128 | bytes 1024 | tf_op jit(solution)/shard_map/optimization_barrier | solution.py:158
  66.5 0.0 collective-permute-done.5
  66.5 0.0 collective-permute-done.4
  66.5 0.8 copy-done.1
  67.3 0.0 collective-permute-done.3
  67.3 1.4 %pad_maximum_fusion.mine = f32[16,264,128]{2,1,0:T(8,128)S(1)} fusion(f32[4,264,128]{2,1,0:T(8,128)S(1)} %collective-permute-done.5, f32[4,264,128]{2,1,0:T(8,128)} %copy-done.1, f32[4,264,128]{2,1,0:T(8,128)} %collective-permute-done.3, f32[4,264,128]{2,1,0:T(8,128)S(1)} %pad_maximum_fusion.1), kind=kLoop, calls=%fused_computation | loop fusion | flops 1622016 | bytes 4325376 | tf_op jit(solution)/shard_map/concatenate | solution.py:157
  68.7 0.0 copy-start
  68.7 1.9 %collective-permute-start.6 = (f32[16,264,128]{2,1,0:T(8,128)S(1)}, f32[16,264,128]{2,1,0:T(8,128)}, u32[]{:S(2)}, u32[]{:S(2)}) collective-permute-start(f32[16,264,128]{2,1,0:T(8,128)S(1)} %pad_maximum_fusion.mine), channel_id=1, source_target_pairs={{0,16},{16,0},{32,48},{48,32},{64,80},{80,64},{96,112},{112,96},{1... | collective-permute-start | bytes 6488072 | tf_op jit(solution)/shard_map/ppermute | solution.py:31
  70.6 0.6 pad_add_fusion.me
  71.2 3.7 %collective-permute-done.6.other = f32[16,264,128]{2,1,0:T(8,128)} collective-permute-done((f32[16,264,128]{2,1,0:T(8,128)S(1)}, f32[16,264,128]{2,1,0:T(8,128)}, u32[]{:S(2)}, u32[]{:S(2)}) %collective-permute-start.6) | collective-permute-done | bytes 2162720 | tf_op jit(solution)/shard_map/ppermute | solution.py:31
  74.9 5.3 %shard_map.46.todo = s32[6,68]{1,0:T(8,128)} custom-call(s32[3]{0:T(128)} %pad_add_fusion.me, s32[128]{0:T(128)} %all-reduce.1.l_where, f32[16,264,128]{2,1,0:T(8,128)} %copy-done, f32[16,264,128]{2,1,0:T(8,128)} %collective-permute-done.6.other), custom_call_target="tpu_custom_call" | custom-call | tf_op jit(solution)/shard_map/pallas_call | solution.py:124
  80.2 12.7 %all-gather.2.cloned.1.call-done.left = f32[16,512,128]{2,1,0:T(8,128)} async-done(((f32[1,512,128]{2,1,0:T(8,128)}), f32[16,512,128]{2,1,0:T(8,128)}) %all-gather.2.cloned.1.call-update) | async-done | bytes 4194320 | tf_op jit(solution)/shard_map/all_gather | solution.py:152
  92.9 6.1 %shard_map.47 = f32[512,512]{1,0:T(8,128)} custom-call(s32[6,68]{1,0:T(8,128)} %shard_map.46.todo, f32[16,512,128]{2,1,0:T(8,128)} %all-gather.2.cloned.1.call-done.left, f32[16,264,128]{2,1,0:T(8,128)} %copy-done, f32[16,264,128]{2,1,0:T(8,128)} %collective-permute-done.6.other), custom_call_target="tpu_custom_call" | custom-call | tf_op jit(solution)/shard_map/pallas_call | solution.py:135
  (4 shorter events, 0.0 us)
Async XLA Ops:
  6.5 86.4 %all-gather.2.cloned.1.call-start = ((), (), s32[]{:S(2)}) async-start(), calls=%async_computation | async-start | bytes 4456448 | tf_op jit(solution)/shard_map/all_gather | solution.py:152
  9.0 12.5 %collective-permute-start.1 = (f32[264,128]{1,0:T(8,128)S(1)}, f32[264,128]{1,0:T(8,128)S(1)}, u32[]{:S(2)}, u32[]{:S(2)}) collective-permute-start(f32[264,128]{1,0:T(8,128)S(1)} %get-tuple-element.14), channel_id=1, source_target_pairs={{0,256},{16,272},{32,288},{48,304},{64,320},{80,336},{96,352},{112... | collective-permute-start | bytes 405512 | tf_op jit(solution)/shard_map/ppermute | solution.py:31
  12.3 10.2 %collective-permute-start = (f32[264,128]{1,0:T(8,128)S(1)}, f32[264,128]{1,0:T(8,128)S(1)}, u32[]{:S(2)}, u32[]{:S(2)}) collective-permute-start(f32[264,128]{1,0:T(8,128)S(1)} %get-tuple-element.14), channel_id=1, source_target_pairs={{0,128},{16,144},{32,160},{48,176},{64,192},{80,208},{96,224},{112... | collective-permute-start | bytes 405512 | tf_op jit(solution)/shard_map/ppermute | solution.py:31
  18.7 8.1 %collective-permute-start.2 = (f32[264,128]{1,0:T(8,128)S(1)}, f32[264,128]{1,0:T(8,128)S(1)}, u32[]{:S(2)}, u32[]{:S(2)}) collective-permute-start(f32[264,128]{1,0:T(8,128)S(1)} %get-tuple-element.14), channel_id=1, source_target_pairs={{0,384},{16,400},{32,416},{48,432},{64,448},{80,464},{96,480},{112... | collective-permute-start | bytes 405512 | tf_op jit(solution)/shard_map/ppermute | solution.py:31
  26.8 39.7 %collective-permute-start.5 = (f32[4,264,128]{2,1,0:T(8,128)S(1)}, f32[4,264,128]{2,1,0:T(8,128)S(1)}, u32[]{:S(2)}, u32[]{:S(2)}) collective-permute-start(f32[4,264,128]{2,1,0:T(8,128)S(1)} %pad_maximum_fusion.1), channel_id=1, source_target_pairs={{0,96},{16,112},{32,0},{48,16},{64,32},{80,48},{96,64},{112,80},{1... | collective-permute-start | bytes 1622024 | tf_op jit(solution)/shard_map/ppermute | solution.py:31
  29.4 37.1 %collective-permute-start.4 = (f32[4,264,128]{2,1,0:T(8,128)S(1)}, f32[4,264,128]{2,1,0:T(8,128)S(1)}, u32[]{:S(2)}, u32[]{:S(2)}) collective-permute-start(f32[4,264,128]{2,1,0:T(8,128)S(1)} %pad_maximum_fusion.1), channel_id=1, source_target_pairs={{0,64},{16,80},{32,96},{48,112},{64,0},{80,16},{96,32},{112,48},{1... | collective-permute-start | bytes 1622024 | tf_op jit(solution)/shard_map/ppermute | solution.py:31
  31.9 35.4 %collective-permute-start.3 = (f32[4,264,128]{2,1,0:T(8,128)S(1)}, f32[4,264,128]{2,1,0:T(8,128)}, u32[]{:S(2)}, u32[]{:S(2)}) collective-permute-start(f32[4,264,128]{2,1,0:T(8,128)S(1)} %pad_maximum_fusion.1), channel_id=1, source_target_pairs={{0,32},{16,48},{32,64},{48,80},{64,96},{80,112},{96,0},{112,16},{1... | collective-permute-start | bytes 1622024 | tf_op jit(solution)/shard_map/ppermute | solution.py:31
  66.5 0.8 copy-start.1
  68.7 6.3 %copy-start = (f32[16,264,128]{2,1,0:T(8,128)}, f32[16,264,128]{2,1,0:T(8,128)S(1)}, u32[]{:S(2)}) copy-start(f32[16,264,128]{2,1,0:T(8,128)S(1)} %pad_maximum_fusion.mine) | copy-start | bytes 6488068
  68.7 6.3 %collective-permute-start.6 = (f32[16,264,128]{2,1,0:T(8,128)S(1)}, f32[16,264,128]{2,1,0:T(8,128)}, u32[]{:S(2)}, u32[]{:S(2)}) collective-permute-start(f32[16,264,128]{2,1,0:T(8,128)S(1)} %pad_maximum_fusion.mine), channel_id=1, source_target_pairs={{0,16},{16,0},{32,48},{48,32},{64,80},{80,64},{96,112},{112,96},{1... | collective-permute-start | bytes 6488072 | tf_op jit(solution)/shard_map/ppermute | solution.py:31
Sparse Core Ops, SparseCore 0:
  9.4 83.4 all-gather.1

commit v3 on v2

v3 whole, which is shorter than its diff:
```python
import jax
import jax.numpy as jnp
from jax import lax
from jax.experimental import pallas as pl
from jax.experimental.pallas import tpu as pltpu
from jax.sharding import PartitionSpec as P

BS = 128
STEPS = 2
BR = 4
BC = 4
LCAP = 2
N_ROW = 32
N_COL = 16
SIDE = 4
AREA = SIDE * SIDE
SLOTS = STEPS * LCAP
UNROLL = 4
LIMIT = 60
MOST = N_COL * SLOTS
F32 = jnp.float32
I32 = jnp.int32


def along_row(x, dx, dy, dc):
    pairs = []
    for r in range(N_ROW):
        a, b, c = r // (2 * SIDE), r // 2 % SIDE, r % 2
        to = ((a + dx) % SIDE * SIDE + (b + dy) % SIDE) * 2 + (c ^ dc)
        pairs.append((r, to))
    return lax.ppermute(x, "row", pairs)


def packed(blocks, index):
    where = index.reshape(1, -1).astype(F32)
    where = jnp.pad(where, ((0, 7), (0, BS - where.shape[1])))
    return jnp.concatenate([blocks.reshape(-1, BS), where], axis=0)


def split(x):
    high = x.astype(jnp.bfloat16)
    return high, (x - high.astype(F32)).astype(jnp.bfloat16)


def match_kernel(me, l_where, mine, other, todo, staged, r_buf, r_where, sem):
    copies = []
    for h, ref in enumerate((mine, other)):
        tile = ref.at[:, pl.ds(STEPS * BS, 8)]
        copies.append(pltpu.make_async_copy(tile, r_where.at[h], sem.at[h]))
    for h, ref in enumerate((mine, other)):
        half = r_buf.at[pl.ds(h * AREA, AREA)]
        copies.append(pltpu.make_async_copy(ref, half, sem.at[2 + h]))
    for copy in copies:
        copy.start()
    copies[0].wait()
    copies[1].wait()

    def look(u, count):
        for s in range(STEPS):
            for t in range(LCAP):
                i = l_where[u * 2 * SLOTS + s * 2 * LCAP + t]
                k = jnp.clip(l_where[u * 2 * SLOTS + s * 2 * LCAP + LCAP + t], 0, N_ROW - 1)
                dx = (me[0] + SIDE - lax.shift_right_logical(k, 3)) & (SIDE - 1)
                dy = (me[1] + SIDE - (lax.shift_right_logical(k, 1) & (SIDE - 1))) & (SIDE - 1)
                half = (me[2] + k) & 1
                place = dy * SIDE + dx
                row = r_where[half, place, 0, s * 2].astype(I32)
                j = r_where[half, place, 0, s * 2 + 1].astype(I32)
                todo[0, count] = u
                todo[1, count] = (s * LCAP + t) * BS
                todo[2, count] = half * AREA + place
                todo[3, count] = s * BS
                todo[4, count] = i * BC + j
                count = count + ((i >= 0) & (row == k)).astype(I32)
        return count

    count = lax.fori_loop(0, N_COL, look, jnp.int32(0))
    copies[2].wait()
    copies[3].wait()

    def stage(n, carry):
        rows = pl.ds(pl.multiple_of(todo[3, n], BS), BS)
        staged[n] = jnp.concatenate(split(r_buf[todo[2, n], rows, :]), axis=1)
        return carry

    lax.fori_loop(0, count, stage, 0)
    for n in range(UNROLL - 1):
        staged[count + n] = jnp.zeros(staged.shape[1:], staged.dtype)
        for field in range(5):
            todo[field, count + n] = 0
    todo[5, 0] = count


def product_kernel(todo, left, staged, out_ref, l_buf, r_buf, sem, r_sem):
    steps = lax.div(todo[5, 0] + UNROLL - 1, UNROLL)

    def fetch(n):
        rows = pl.ds(pl.multiple_of(todo[1, n], BS), BS)
        return pltpu.make_async_copy(left.at[todo[0, n], rows], l_buf.at[n], sem.at[n])

    def fetch_staged(step):
        some = pl.ds(step * UNROLL, UNROLL)
        return pltpu.make_async_copy(staged.at[some], r_buf.at[some], r_sem.at[step])

    def start(step, carry):
        for n in range(UNROLL):
            fetch(step * UNROLL + n).start()
        fetch_staged(step).start()
        return carry

    lax.fori_loop(0, steps, start, 0)
    out_ref[...] = jnp.zeros_like(out_ref)

    def multiply(step, carry):
        for n in range(UNROLL):
            fetch(step * UNROLL + n).wait()
        fetch_staged(step).wait()
        sums = []
        for n in range(UNROLL):
            at = step * UNROLL + n
            a = jnp.concatenate(split(l_buf[at]), axis=1)
            b = r_buf[at]
            both = jnp.dot(a, jnp.concatenate([b, b], axis=0), preferred_element_type=F32)
            sums.append(both[:, :BS] + both[:, BS:])
        for n in range(UNROLL):
            at = todo[4, step * UNROLL + n]
            rows = pl.ds(pl.multiple_of(lax.shift_right_logical(at, 2) * BS, BS), BS)
            cols = pl.ds(pl.multiple_of((at & (BC - 1)) * BS, BS), BS)
            out_ref[rows, cols] += sums[n]
        return carry

    lax.fori_loop(0, steps, multiply, 0)


HBM = pl.BlockSpec(memory_space=pltpu.HBM)
SMEM = pl.BlockSpec(memory_space=pltpu.SMEM)


VMEM = pl.BlockSpec(memory_space=pltpu.VMEM)
ROOM = pltpu.CompilerParams(vmem_limit_bytes=LIMIT * 1024 * 1024)


def matches(me, l_where, mine, other):
    return pl.pallas_call(
        match_kernel,
        out_shape=[
            jax.ShapeDtypeStruct((6, MOST + UNROLL), I32),
            jax.ShapeDtypeStruct((MOST + UNROLL, BS, 2 * BS), jnp.bfloat16),
        ],
        in_specs=[SMEM, SMEM, HBM, HBM],
        out_specs=[SMEM, VMEM],
        scratch_shapes=[
            pltpu.VMEM((2 * AREA,) + mine.shape[1:], F32),
            pltpu.SMEM((2, AREA, 8, BS), F32),
            pltpu.SemaphoreType.DMA((4,)),
        ],
        compiler_params=ROOM,
    )(me, l_where, mine, other)


def products(todo, left, staged):
    return pl.pallas_call(
        product_kernel,
        out_shape=jax.ShapeDtypeStruct((BR * BS, BC * BS), F32),
        in_specs=[SMEM, HBM, HBM],
        out_specs=VMEM,
        scratch_shapes=[
            pltpu.VMEM((MOST + UNROLL, BS, BS), F32),
            pltpu.VMEM(staged.shape, staged.dtype),
            pltpu.SemaphoreType.DMA((MOST + UNROLL,)),
            pltpu.SemaphoreType.DMA((MOST // UNROLL,)),
        ],
        compiler_params=ROOM,
    )(todo, left, staged)


def per_device(left_blocks, left_index, right_blocks, right_index):
    left = lax.all_gather(left_blocks.reshape(SLOTS * BS, BS), "col", axis=0)
    mine = packed(right_blocks, right_index)
    line = jnp.stack([mine, *[along_row(mine, d, 0, 0) for d in (1, 2, 3)]])
    l_index, line = lax.optimization_barrier((left_index, line))
    l_where = lax.all_gather(l_index.reshape(-1), "col", axis=0, tiled=True)
    area = jnp.concatenate([line, *[along_row(line, 0, d, 0) for d in (1, 2, 3)]])
    area, l_where = lax.optimization_barrier((area, l_where))
    other = along_row(area, 0, 0, 1)
    row = lax.axis_index("row")
    me = jnp.stack([row // (2 * SIDE), row // 2 % SIDE, row % 2]).astype(I32)
    todo, staged = matches(me, l_where, area, other)
    return products(todo, left, staged)


def solution(mesh):
    placed = (
        P(None, "row", "col", None, None),
        P(None, None, "row", "col"),
        P(None, "row", "col", None, None),
        P(None, None, "row", "col"),
    )
    return jax.shard_map(
        per_device, mesh=mesh, in_specs=placed, out_specs=P("row", "col"), check_vma=False
    )
```

time: 107 us -> 105 us (0.981)
  waiting for transfers between devices: 22.4 us -> 20.1 us
    all_gather x1, waiting for transfers between devices: 12.7 us -> 10.4 us  [per_device(): left = lax.all_gather(left_blocks.reshape(SLOTS * BS, BS), 'col', axis=0)]
    pallas_call x1, Pallas kernels: 5.27 us -> 7.06 us  [matches(): pl.pallas_call(match_kernel, out_shape=[jax.ShapeDtypeStruct((6, MOST + U...]
    pallas_call x1, Pallas kernels: 6.14 us -> 4.8 us  [products(): pl.pallas_call(product_kernel, out_shape=jax.ShapeDtypeStruct((BR * BS, B...]
  transfers between devices with their start and end apart: 8 -> 8, of which waited for: 4 -> 4; matrix products, arithmetic and copies ran while one was open for 7% -> 7% of each run, Pallas kernels for 5% -> 7%
where the time goes in v3:
time: 105 us
  blocking collectives  27 us (26%)
  starting transfers between devices  23.3 us (22%)
  waiting for transfers between devices  20.1 us (19%)
  between operations  14.2 us (14%)
  Pallas kernels  11.9 us (11%)
  other arithmetic  5 us (5%)
  local copies, waits for them, and re-layouts  2.94 us (3%)
    optimization_barrier x1, blocking collectives, per_device(): area, l_where = lax.optimization_barrier((area, l_where))  27 us
    ppermute x7, starting transfers between devices, along_row(): return lax.ppermute(x, 'row', pairs)  23.3 us
    all_gather x1, waiting for transfers between devices, per_device(): left = lax.all_gather(left_blocks.reshape(SLOTS * BS, BS), 'col', axis=0)  10.4 us
    ppermute x7, waiting for transfers between devices, along_row(): return lax.ppermute(x, 'row', pairs)  9.03 us
    pallas_call x1, Pallas kernels, matches(): pl.pallas_call(match_kernel, out_shape=[jax.ShapeDtypeStruct((6, MOST + U...  7.06 us
    pallas_call x1, Pallas kernels, products(): pl.pallas_call(product_kernel, out_shape=jax.ShapeDtypeStruct((BR * BS, B...  4.8 us
    unnamed x7, local copies, waits for them, and re-layouts  2.26 us
  transfers between devices with their start and end apart: 8, of which 4 were waited for; matrix products, arithmetic and copies ran while one was open for 7% of the time, Pallas kernels for 7%

profile of v3, /device:TPU:6, one launch (start us, length us, event | category | flops | bytes accessed | tf_op | source)
XLA Modules:
  0.0 104.5 jit_solution(7650851434805571024)
XLA Ops:
  6.5 0.7 all-gather.2.cloned.1.call-update
  7.3 0.7 convert_reduce_fusion
  8.0 0.1 convert_element_type.17
  8.0 0.9 fusion
  9.0 7.8 %collective-permute-start = (f32[264,128]{1,0:T(8,128)S(1)}, f32[264,128]{1,0:T(8,128)S(1)}, u32[]{:S(2)}, u32[]{:S(2)}) collective-permute-start(f32[264,128]{1,0:T(8,128)S(1)} %get-tuple-element.18), channel_id=1, source_target_pairs={{0,128},{16,144},{32,160},{48,176},{64,192},{80,208},{96,224},{112... | collective-permute-start | bytes 405512 | tf_op jit(solution)/shard_map/ppermute | solution.py:31
  16.7 1.9 %collective-permute-start.1 = (f32[264,128]{1,0:T(8,128)S(1)}, f32[264,128]{1,0:T(8,128)S(1)}, u32[]{:S(2)}, u32[]{:S(2)}) collective-permute-start(f32[264,128]{1,0:T(8,128)S(1)} %get-tuple-element.18), channel_id=1, source_target_pairs={{0,256},{16,272},{32,288},{48,304},{64,320},{80,336},{96,352},{112... | collective-permute-start | bytes 405512 | tf_op jit(solution)/shard_map/ppermute | solution.py:31
  18.7 2.8 %collective-permute-start.2 = (f32[264,128]{1,0:T(8,128)S(1)}, f32[264,128]{1,0:T(8,128)S(1)}, u32[]{:S(2)}, u32[]{:S(2)}) collective-permute-start(f32[264,128]{1,0:T(8,128)S(1)} %get-tuple-element.18), channel_id=1, source_target_pairs={{0,384},{16,400},{32,416},{48,432},{64,448},{80,464},{96,480},{112... | collective-permute-start | bytes 405512 | tf_op jit(solution)/shard_map/ppermute | solution.py:31
  21.4 0.0 collective-permute-done
  21.4 3.7 %collective-permute-done.1 = f32[264,128]{1,0:T(8,128)S(1)} collective-permute-done((f32[264,128]{1,0:T(8,128)S(1)}, f32[264,128]{1,0:T(8,128)S(1)}, u32[]{:S(2)}, u32[]{:S(2)}) %collective-permute-start.1) | collective-permute-done | bytes 135200 | tf_op jit(solution)/shard_map/ppermute | solution.py:31
  25.1 1.6 %collective-permute-done.2 = f32[264,128]{1,0:T(8,128)S(1)} collective-permute-done((f32[264,128]{1,0:T(8,128)S(1)}, f32[264,128]{1,0:T(8,128)S(1)}, u32[]{:S(2)}, u32[]{:S(2)}) %collective-permute-start.2) | collective-permute-done | bytes 135200 | tf_op jit(solution)/shard_map/ppermute | solution.py:31
  26.8 0.1 pad_maximum_fusion.1
  26.8 1.9 %collective-permute-start.3 = (f32[4,264,128]{2,1,0:T(8,128)S(1)}, f32[4,264,128]{2,1,0:T(8,128)S(1)}, u32[]{:S(2)}, u32[]{:S(2)}) collective-permute-start(f32[4,264,128]{2,1,0:T(8,128)S(1)} %pad_maximum_fusion.1), channel_id=1, source_target_pairs={{0,32},{16,48},{32,64},{48,80},{64,96},{80,112},{96,0},{112,16},{1... | collective-permute-start | bytes 1622024 | tf_op jit(solution)/shard_map/ppermute | solution.py:31
  28.8 3.4 %collective-permute-start.4 = (f32[4,264,128]{2,1,0:T(8,128)S(1)}, f32[4,264,128]{2,1,0:T(8,128)S(1)}, u32[]{:S(2)}, u32[]{:S(2)}) collective-permute-start(f32[4,264,128]{2,1,0:T(8,128)S(1)} %pad_maximum_fusion.1), channel_id=1, source_target_pairs={{0,64},{16,80},{32,96},{48,112},{64,0},{80,16},{96,32},{112,48},{1... | collective-permute-start | bytes 1622024 | tf_op jit(solution)/shard_map/ppermute | solution.py:31
  32.2 3.6 %collective-permute-start.5 = (f32[4,264,128]{2,1,0:T(8,128)S(1)}, f32[4,264,128]{2,1,0:T(8,128)}, u32[]{:S(2)}, u32[]{:S(2)}) collective-permute-start(f32[4,264,128]{2,1,0:T(8,128)S(1)} %pad_maximum_fusion.1), channel_id=1, source_target_pairs={{0,96},{16,112},{32,0},{48,16},{64,32},{80,48},{96,64},{112,80},{1... | collective-permute-start | bytes 1622024 | tf_op jit(solution)/shard_map/ppermute | solution.py:31
  35.8 1.3 %dynamic-slice = u32[1]{0:T(128)} dynamic-slice(u32[512]{0:T(512)} %constant.61, u32[]{:T(128)S(6)} %add.13), dynamic_slice_sizes={1} | dynamic-slice | bytes 12
  37.8 0.5 broadcast.21
  38.3 1.3 %reduce.7 = s32[2,2,2]{2,1,0:T(2,128)S(1)} reduce(s32[2,2,1,2]{3,2,1,0:T(1,128)} %param.5, s32[]{:T(128)} %broadcast.21), dimensions={2}, to_apply=%get-tuple-element.12.reduce_sub_computation.3 | reduce | bytes 68 | tf_op jit(solution)/shard_map/optimization_barrier | solution.py:181
  39.6 0.1 reshape.22
  39.7 0.2 dynamic-update-slice
  39.9 27.0 %all-reduce.1.l_where = s32[128]{0:T(128)} all-reduce(s32[128]{0:T(128)S(1)} %dynamic-update-slice), channel_id=1, replica_groups=mesh['row'=32,'col'=16] {'col'}, use_global_device_ids=true, to_apply=%add.1 | all-reduce | flops 128 | bytes 1024 | tf_op jit(solution)/shard_map/optimization_barrier | solution.py:184
  66.9 0.0 collective-permute-done.3
  66.9 0.0 collective-permute-done.4
  66.9 0.8 copy-done.1
  67.7 0.0 collective-permute-done.5
  67.7 1.4 %pad_maximum_fusion.mine = f32[16,264,128]{2,1,0:T(8,128)S(1)} fusion(f32[4,264,128]{2,1,0:T(8,128)} %collective-permute-done.5, f32[4,264,128]{2,1,0:T(8,128)} %copy-done.1, f32[4,264,128]{2,1,0:T(8,128)S(1)} %collective-permute-done.3, f32[4,264,128]{2,1,0:T(8,128)S(1)} %pad_maximum_fusion.1), kind=kLoop, calls=%fused_computation | loop fusion | flops 1622016 | bytes 4325376 | tf_op jit(solution)/shard_map/concatenate | solution.py:183
  69.1 1.9 %collective-permute-start.6 = (f32[16,264,128]{2,1,0:T(8,128)S(1)}, f32[16,264,128]{2,1,0:T(8,128)}, u32[]{:S(2)}, u32[]{:S(2)}) collective-permute-start(f32[16,264,128]{2,1,0:T(8,128)S(1)} %pad_maximum_fusion.mine), channel_id=1, source_target_pairs={{0,16},{16,0},{32,48},{48,32},{64,80},{80,64},{96,112},{112,96},{1... | collective-permute-start | bytes 6488072 | tf_op jit(solution)/shard_map/ppermute | solution.py:31
  71.1 0.6 pad_add_fusion.me
  71.7 3.7 %collective-permute-done.6.other = f32[16,264,128]{2,1,0:T(8,128)} collective-permute-done((f32[16,264,128]{2,1,0:T(8,128)S(1)}, f32[16,264,128]{2,1,0:T(8,128)}, u32[]{:S(2)}, u32[]{:S(2)}) %collective-permute-start.6) | collective-permute-done | bytes 2162720 | tf_op jit(solution)/shard_map/ppermute | solution.py:31
  75.4 0.0 copy-done
  75.4 7.1 %shard_map.46 = (s32[6,68]{1,0:T(8,128)}, bf16[68,128,256]{2,1,0:T(8,128)(2,1)}) custom-call(s32[3]{0:T(128)} %pad_add_fusion.me, s32[128]{0:T(128)} %all-reduce.1.l_where, f32[16,264,128]{2,1,0:T(8,128)} %copy-done, f32[16,264,128]{2,1,0:T(8,128)} %collective-permute-done.6.other), custom_call_target="tpu_custom_call" | custom-call | tf_op jit(solution)/shard_map/pallas_call | solution.py:144
  82.4 10.4 %all-gather.2.cloned.1.call-done.left = f32[16,512,128]{2,1,0:T(8,128)} async-done(((f32[1,512,128]{2,1,0:T(8,128)}), f32[16,512,128]{2,1,0:T(8,128)}) %all-gather.2.cloned.1.call-update) | async-done | bytes 4194320 | tf_op jit(solution)/shard_map/all_gather | solution.py:178
  92.8 4.8 %shard_map.47 = f32[512,512]{1,0:T(8,128)} custom-call(s32[6,68]{1,0:T(8,128)} %get-tuple-element.15.todo, f32[16,512,128]{2,1,0:T(8,128)} %all-gather.2.cloned.1.call-done.left, bf16[68,128,256]{2,1,0:T(8,128)(2,1)} %get-tuple-element.16.staged), custom_call_target="tpu_custom_call" | custom-call | tf_op jit(solution)/shard_map/pallas_call | solution.py:162
  (4 shorter events, 0.0 us)
Async XLA Ops:
  6.5 86.3 %all-gather.2.cloned.1.call-start = ((), (), s32[]{:S(2)}) async-start(), calls=%async_computation | async-start | bytes 4456448 | tf_op jit(solution)/shard_map/all_gather | solution.py:178
  9.0 12.5 %collective-permute-start = (f32[264,128]{1,0:T(8,128)S(1)}, f32[264,128]{1,0:T(8,128)S(1)}, u32[]{:S(2)}, u32[]{:S(2)}) collective-permute-start(f32[264,128]{1,0:T(8,128)S(1)} %get-tuple-element.18), channel_id=1, source_target_pairs={{0,128},{16,144},{32,160},{48,176},{64,192},{80,208},{96,224},{112... | collective-permute-start | bytes 405512 | tf_op jit(solution)/shard_map/ppermute | solution.py:31
  16.7 8.4 %collective-permute-start.1 = (f32[264,128]{1,0:T(8,128)S(1)}, f32[264,128]{1,0:T(8,128)S(1)}, u32[]{:S(2)}, u32[]{:S(2)}) collective-permute-start(f32[264,128]{1,0:T(8,128)S(1)} %get-tuple-element.18), channel_id=1, source_target_pairs={{0,256},{16,272},{32,288},{48,304},{64,320},{80,336},{96,352},{112... | collective-permute-start | bytes 405512 | tf_op jit(solution)/shard_map/ppermute | solution.py:31
  18.7 8.1 %collective-permute-start.2 = (f32[264,128]{1,0:T(8,128)S(1)}, f32[264,128]{1,0:T(8,128)S(1)}, u32[]{:S(2)}, u32[]{:S(2)}) collective-permute-start(f32[264,128]{1,0:T(8,128)S(1)} %get-tuple-element.18), channel_id=1, source_target_pairs={{0,384},{16,400},{32,416},{48,432},{64,448},{80,464},{96,480},{112... | collective-permute-start | bytes 405512 | tf_op jit(solution)/shard_map/ppermute | solution.py:31
  26.8 40.1 %collective-permute-start.3 = (f32[4,264,128]{2,1,0:T(8,128)S(1)}, f32[4,264,128]{2,1,0:T(8,128)S(1)}, u32[]{:S(2)}, u32[]{:S(2)}) collective-permute-start(f32[4,264,128]{2,1,0:T(8,128)S(1)} %pad_maximum_fusion.1), channel_id=1, source_target_pairs={{0,32},{16,48},{32,64},{48,80},{64,96},{80,112},{96,0},{112,16},{1... | collective-permute-start | bytes 1622024 | tf_op jit(solution)/shard_map/ppermute | solution.py:31
  28.8 38.2 %collective-permute-start.4 = (f32[4,264,128]{2,1,0:T(8,128)S(1)}, f32[4,264,128]{2,1,0:T(8,128)S(1)}, u32[]{:S(2)}, u32[]{:S(2)}) collective-permute-start(f32[4,264,128]{2,1,0:T(8,128)S(1)} %pad_maximum_fusion.1), channel_id=1, source_target_pairs={{0,64},{16,80},{32,96},{48,112},{64,0},{80,16},{96,32},{112,48},{1... | collective-permute-start | bytes 1622024 | tf_op jit(solution)/shard_map/ppermute | solution.py:31
  32.2 35.5 %collective-permute-start.5 = (f32[4,264,128]{2,1,0:T(8,128)S(1)}, f32[4,264,128]{2,1,0:T(8,128)}, u32[]{:S(2)}, u32[]{:S(2)}) collective-permute-start(f32[4,264,128]{2,1,0:T(8,128)S(1)} %pad_maximum_fusion.1), channel_id=1, source_target_pairs={{0,96},{16,112},{32,0},{48,16},{64,32},{80,48},{96,64},{112,80},{1... | collective-permute-start | bytes 1622024 | tf_op jit(solution)/shard_map/ppermute | solution.py:31
  66.9 0.8 copy-start.1
  69.1 6.3 %copy-start = (f32[16,264,128]{2,1,0:T(8,128)}, f32[16,264,128]{2,1,0:T(8,128)S(1)}, u32[]{:S(2)}) copy-start(f32[16,264,128]{2,1,0:T(8,128)S(1)} %pad_maximum_fusion.mine) | copy-start | bytes 6488068
  69.1 6.3 %collective-permute-start.6 = (f32[16,264,128]{2,1,0:T(8,128)S(1)}, f32[16,264,128]{2,1,0:T(8,128)}, u32[]{:S(2)}, u32[]{:S(2)}) collective-permute-start(f32[16,264,128]{2,1,0:T(8,128)S(1)} %pad_maximum_fusion.mine), channel_id=1, source_target_pairs={{0,16},{16,0},{32,48},{48,32},{64,80},{80,64},{96,112},{112,96},{1... | collective-permute-start | bytes 6488072 | tf_op jit(solution)/shard_map/ppermute | solution.py:31
Sparse Core Ops, SparseCore 0:
  9.4 83.3 all-gather.1

commit v4 on v3

--- a/solution.py
+++ b/solution.py
@@ -16,6 +16,8 @@
 AREA = SIDE * SIDE
 SLOTS = STEPS * LCAP
 UNROLL = 4
+REST = 112
+MAIN = SLOTS * BS - REST
 LIMIT = 60
 MOST = N_COL * SLOTS
 F32 = jnp.float32
@@ -42,8 +44,8 @@
     return high, (x - high.astype(F32)).astype(jnp.bfloat16)
 
 
-def match_kernel(me, l_where, mine, other, todo, staged, r_buf, r_where, sem):
-    copies = []
+def match_kernel(me, rest, mine, other, todo, staged, r_buf, l_where, r_where, sem):
+    copies = [pltpu.make_async_copy(rest.at[:, pl.ds(REST, 8)], l_where, sem.at[4])]
     for h, ref in enumerate((mine, other)):
         tile = ref.at[:, pl.ds(STEPS * BS, 8)]
         copies.append(pltpu.make_async_copy(tile, r_where.at[h], sem.at[h]))
@@ -52,14 +54,14 @@
         copies.append(pltpu.make_async_copy(ref, half, sem.at[2 + h]))
     for copy in copies:
         copy.start()
-    copies[0].wait()
-    copies[1].wait()
+    for copy in copies[:3]:
+        copy.wait()
 
     def look(u, count):
         for s in range(STEPS):
             for t in range(LCAP):
-                i = l_where[u * 2 * SLOTS + s * 2 * LCAP + t]
-                k = jnp.clip(l_where[u * 2 * SLOTS + s * 2 * LCAP + LCAP + t], 0, N_ROW - 1)
+                i = l_where[u, 0, s * 2 * LCAP + t].astype(I32)
+                k = jnp.clip(l_where[u, 0, s * 2 * LCAP + LCAP + t].astype(I32), 0, N_ROW - 1)
                 dx = (me[0] + SIDE - lax.shift_right_logical(k, 3)) & (SIDE - 1)
                 dy = (me[1] + SIDE - (lax.shift_right_logical(k, 1) & (SIDE - 1))) & (SIDE - 1)
                 half = (me[2] + k) & 1
@@ -75,8 +77,8 @@
         return count
 
     count = lax.fori_loop(0, N_COL, look, jnp.int32(0))
-    copies[2].wait()
     copies[3].wait()
+    copies[4].wait()
 
     def stage(n, carry):
         rows = pl.ds(pl.multiple_of(todo[3, n], BS), BS)
@@ -91,12 +93,28 @@
     todo[5, 0] = count
 
 
-def product_kernel(todo, left, staged, out_ref, l_buf, r_buf, sem, r_sem):
+def product_kernel(todo, left, rest, staged, out_ref, l_buf, r_buf, sem, r_sem):
     steps = lax.div(todo[5, 0] + UNROLL - 1, UNROLL)
 
     def fetch(n):
-        rows = pl.ds(pl.multiple_of(todo[1, n], BS), BS)
-        return pltpu.make_async_copy(left.at[todo[0, n], rows], l_buf.at[n], sem.at[n])
+        u, first = todo[0, n], todo[1, n]
+        split_slot = first + BS > MAIN
+
+        @pl.when(jnp.logical_not(split_slot))
+        def _():
+            rows = pl.ds(pl.multiple_of(first, BS), BS)
+            pltpu.make_async_copy(left.at[u, rows], l_buf.at[n], sem.at[n]).start()
+
+        @pl.when(split_slot)
+        def _():
+            head = pl.ds(MAIN - (BS - REST), BS - REST)
+            to = l_buf.at[n, pl.ds(0, BS - REST)]
+            pltpu.make_async_copy(left.at[u, head], to, sem.at[n]).start()
+            to = l_buf.at[n, pl.ds(BS - REST, REST)]
+            pltpu.make_async_copy(rest.at[u, pl.ds(0, REST)], to, sem.at[n]).start()
+
+    def fetched(n):
+        return pltpu.make_async_copy(left.at[0, pl.ds(0, BS)], l_buf.at[n], sem.at[n])
 
     def fetch_staged(step):
         some = pl.ds(step * UNROLL, UNROLL)
@@ -104,7 +122,7 @@
 
     def start(step, carry):
         for n in range(UNROLL):
-            fetch(step * UNROLL + n).start()
+            fetch(step * UNROLL + n)
         fetch_staged(step).start()
         return carry
 
@@ -113,7 +131,7 @@
 
     def multiply(step, carry):
         for n in range(UNROLL):
-            fetch(step * UNROLL + n).wait()
+            fetched(step * UNROLL + n).wait()
         fetch_staged(step).wait()
         sums = []
         for n in range(UNROLL):
@@ -140,29 +158,30 @@
 ROOM = pltpu.CompilerParams(vmem_limit_bytes=LIMIT * 1024 * 1024)
 
 
-def matches(me, l_where, mine, other):
+def matches(me, rest, mine, other):
     return pl.pallas_call(
         match_kernel,
         out_shape=[
             jax.ShapeDtypeStruct((6, MOST + UNROLL), I32),
             jax.ShapeDtypeStruct((MOST + UNROLL, BS, 2 * BS), jnp.bfloat16),
         ],
-        in_specs=[SMEM, SMEM, HBM, HBM],
+        in_specs=[SMEM, HBM, HBM, HBM],
         out_specs=[SMEM, VMEM],
         scratch_shapes=[
             pltpu.VMEM((2 * AREA,) + mine.shape[1:], F32),
+            pltpu.SMEM((N_COL, 8, BS), F32),
             pltpu.SMEM((2, AREA, 8, BS), F32),
-            pltpu.SemaphoreType.DMA((4,)),
+            pltpu.SemaphoreType.DMA((5,)),
         ],
         compiler_params=ROOM,
-    )(me, l_where, mine, other)
-
-
-def products(todo, left, staged):
+    )(me, rest, mine, other)
+
+
+def products(todo, left, rest, staged):
     return pl.pallas_call(
         product_kernel,
         out_shape=jax.ShapeDtypeStruct((BR * BS, BC * BS), F32),
-        in_specs=[SMEM, HBM, HBM],
+        in_specs=[SMEM, HBM, HBM, HBM],
         out_specs=VMEM,
         scratch_shapes=[
             pltpu.VMEM((MOST + UNROLL, BS, BS), F32),
@@ -171,22 +190,23 @@
             pltpu.SemaphoreType.DMA((MOST // UNROLL,)),
         ],
         compiler_params=ROOM,
-    )(todo, left, staged)
+    )(todo, left, rest, staged)
 
 
 def per_device(left_blocks, left_index, right_blocks, right_index):
-    left = lax.all_gather(left_blocks.reshape(SLOTS * BS, BS), "col", axis=0)
+    left_blocks = left_blocks.reshape(SLOTS * BS, BS)
+    left = lax.all_gather(left_blocks[:MAIN], "col", axis=0)
     mine = packed(right_blocks, right_index)
     line = jnp.stack([mine, *[along_row(mine, d, 0, 0) for d in (1, 2, 3)]])
-    l_index, line = lax.optimization_barrier((left_index, line))
-    l_where = lax.all_gather(l_index.reshape(-1), "col", axis=0, tiled=True)
+    rest, line = lax.optimization_barrier((packed(left_blocks[MAIN:], left_index), line))
+    rest = lax.all_gather(rest, "col", axis=0)
     area = jnp.concatenate([line, *[along_row(line, 0, d, 0) for d in (1, 2, 3)]])
-    area, l_where = lax.optimization_barrier((area, l_where))
+    area, rest = lax.optimization_barrier((area, rest))
     other = along_row(area, 0, 0, 1)
     row = lax.axis_index("row")
     me = jnp.stack([row // (2 * SIDE), row // 2 % SIDE, row % 2]).astype(I32)
-    todo, staged = matches(me, l_where, area, other)
-    return products(todo, left, staged)
+    todo, staged = matches(me, rest, area, other)
+    return products(todo, left, rest, staged)
 
 
 def solution(mesh):

time: 105 us -> 115 us (1.095)
  blocking collectives: 27 us -> 50.1 us
  waiting for transfers between devices: 20.1 us -> 7.43 us
  other arithmetic: 5 us -> 3.18 us
  Pallas kernels: 11.9 us -> 13.1 us
    all_gather x0 -> x1, blocking collectives: none -> 50.1 us  [per_device(): rest = lax.all_gather(rest, 'col', axis=0)]
    optimization_barrier x1 -> x0, blocking collectives: 27 us -> none  [per_device(): area, l_where = lax.optimization_barrier((area, l_where))]
    all_gather x1, waiting for transfers between devices: 10.4 us -> 0.02 us  [per_device(): left = lax.all_gather(left_blocks[:MAIN], 'col', axis=0)]
    slice x0 -> x2, local copies, waits for them, and re-layouts: none -> 2.44 us  [the longest x1 1.62 us: per_device(): left = lax.all_gather(left_blocks[:MAIN], 'col', axis=0)]
    unnamed x7 -> x2, local copies, waits for them, and re-layouts: 2.26 us -> 0.01 us
    ppermute x7, waiting for transfers between devices: 9.03 us -> 7.39 us  [along_row(): return lax.ppermute(x, 'row', pairs)]
    optimization_barrier x1 -> x0, other arithmetic: 1.34 us -> none  [per_device(): l_index, line = lax.optimization_barrier((left_index, line))]
    pallas_call x1, Pallas kernels: 7.06 us -> 8.3 us  [matches(): pl.pallas_call(match_kernel, out_shape=[jax.ShapeDtypeStruct((6, MOST + U...]
  transfers between devices with their start and end apart: 8 -> 8, of which waited for: 4 -> 3; matrix products, arithmetic and copies ran while one was open for 7% -> 4% of each run, Pallas kernels for 7% -> 7%
where the time goes in v4:
time: 115 us; the launch traced here: 113 us
  blocking collectives  50.1 us (44%)
  starting transfers between devices  23.3 us (20%)
  between operations  13.6 us (12%)
  Pallas kernels  13.1 us (11%)
  waiting for transfers between devices  7.43 us (6%)
  other arithmetic  3.18 us (3%)
  local copies, waits for them, and re-layouts  2.62 us (2%)
    all_gather x1, blocking collectives, per_device(): rest = lax.all_gather(rest, 'col', axis=0)  50.1 us
    ppermute x7, starting transfers between devices, along_row(): return lax.ppermute(x, 'row', pairs)  23.3 us
    pallas_call x1, Pallas kernels, matches(): pl.pallas_call(match_kernel, out_shape=[jax.ShapeDtypeStruct((6, MOST + U...  8.3 us
    ppermute x7, waiting for transfers between devices, along_row(): return lax.ppermute(x, 'row', pairs)  7.39 us
    pallas_call x1, Pallas kernels, products(): pl.pallas_call(product_kernel, out_shape=jax.ShapeDtypeStruct((BR * BS, B...  4.82 us
  transfers between devices with their start and end apart: 8, of which 3 were waited for; matrix products, arithmetic and copies ran while one was open for 4% of the time, Pallas kernels for 7%

profile of v4, /device:TPU:6, one launch (start us, length us, event | category | flops | bytes accessed | tf_op | source)
XLA Modules:
  0.0 113.4 jit_solution(16717092155948086495)
XLA Ops:
  6.5 0.0 all-gather.4.cloned.1.call-start
  6.5 1.6 %slice.9 = f32[400,128]{1,0:T(8,128)} slice(f32[512,128]{1,0:T(8,128)} %bitcast.15), slice={[0:400], [0:128]} | slice | bytes 409600 | tf_op jit(solution)/shard_map/slice | solution.py:198
  8.2 0.0 all-gather.4.cloned.1.call-update
  8.2 0.7 convert_reduce_fusion.1
  8.9 0.1 convert_element_type.35
  9.0 0.9 fusion
  9.9 7.8 %collective-permute-start = (f32[264,128]{1,0:T(8,128)S(1)}, f32[264,128]{1,0:T(8,128)S(1)}, u32[]{:S(2)}, u32[]{:S(2)}) collective-permute-start(f32[264,128]{1,0:T(8,128)S(1)} %get-tuple-element.18), channel_id=1, source_target_pairs={{0,128},{16,144},{32,160},{48,176},{64,192},{80,208},{96,224},{112... | collective-permute-start | bytes 405512 | tf_op jit(solution)/shard_map/ppermute | solution.py:33
  17.7 1.9 %collective-permute-start.1 = (f32[264,128]{1,0:T(8,128)S(1)}, f32[264,128]{1,0:T(8,128)S(1)}, u32[]{:S(2)}, u32[]{:S(2)}) collective-permute-start(f32[264,128]{1,0:T(8,128)S(1)} %get-tuple-element.18), channel_id=1, source_target_pairs={{0,256},{16,272},{32,288},{48,304},{64,320},{80,336},{96,352},{112... | collective-permute-start | bytes 405512 | tf_op jit(solution)/shard_map/ppermute | solution.py:33
  19.6 2.8 %collective-permute-start.2 = (f32[264,128]{1,0:T(8,128)S(1)}, f32[264,128]{1,0:T(8,128)S(1)}, u32[]{:S(2)}, u32[]{:S(2)}) collective-permute-start(f32[264,128]{1,0:T(8,128)S(1)} %get-tuple-element.18), channel_id=1, source_target_pairs={{0,384},{16,400},{32,416},{48,432},{64,448},{80,464},{96,480},{112... | collective-permute-start | bytes 405512 | tf_op jit(solution)/shard_map/ppermute | solution.py:33
  22.4 0.7 convert_reduce_fusion
  23.1 0.8 slice.8
  23.9 0.1 convert_element_type.33
  24.0 0.0 collective-permute-done
  24.0 2.1 %collective-permute-done.1 = f32[264,128]{1,0:T(8,128)S(1)} collective-permute-done((f32[264,128]{1,0:T(8,128)S(1)}, f32[264,128]{1,0:T(8,128)S(1)}, u32[]{:S(2)}, u32[]{:S(2)}) %collective-permute-start.1) | collective-permute-done | bytes 135200 | tf_op jit(solution)/shard_map/ppermute | solution.py:33
  26.1 1.6 %collective-permute-done.2 = f32[264,128]{1,0:T(8,128)S(1)} collective-permute-done((f32[264,128]{1,0:T(8,128)S(1)}, f32[264,128]{1,0:T(8,128)S(1)}, u32[]{:S(2)}, u32[]{:S(2)}) %collective-permute-start.2) | collective-permute-done | bytes 135200 | tf_op jit(solution)/shard_map/ppermute | solution.py:33
  27.7 0.1 pad_maximum_fusion.1
  27.8 1.9 %collective-permute-start.3 = (f32[4,264,128]{2,1,0:T(8,128)S(1)}, f32[4,264,128]{2,1,0:T(8,128)S(1)}, u32[]{:S(2)}, u32[]{:S(2)}) collective-permute-start(f32[4,264,128]{2,1,0:T(8,128)S(1)} %pad_maximum_fusion.1), channel_id=1, source_target_pairs={{0,32},{16,48},{32,64},{48,80},{64,96},{80,112},{96,0},{112,16},{1... | collective-permute-start | bytes 1622024 | tf_op jit(solution)/shard_map/ppermute | solution.py:33
  29.7 3.4 %collective-permute-start.4 = (f32[4,264,128]{2,1,0:T(8,128)S(1)}, f32[4,264,128]{2,1,0:T(8,128)S(1)}, u32[]{:S(2)}, u32[]{:S(2)}) collective-permute-start(f32[4,264,128]{2,1,0:T(8,128)S(1)} %pad_maximum_fusion.1), channel_id=1, source_target_pairs={{0,64},{16,80},{32,96},{48,112},{64,0},{80,16},{96,32},{112,48},{1... | collective-permute-start | bytes 1622024 | tf_op jit(solution)/shard_map/ppermute | solution.py:33
  33.1 3.6 %collective-permute-start.5 = (f32[4,264,128]{2,1,0:T(8,128)S(1)}, f32[4,264,128]{2,1,0:T(8,128)S(1)}, u32[]{:S(2)}, u32[]{:S(2)}) collective-permute-start(f32[4,264,128]{2,1,0:T(8,128)S(1)} %pad_maximum_fusion.1), channel_id=1, source_target_pairs={{0,96},{16,112},{32,0},{48,16},{64,32},{80,48},{96,64},{112,80},{1... | collective-permute-start | bytes 1622024 | tf_op jit(solution)/shard_map/ppermute | solution.py:33
  36.8 50.1 %all-gather = f32[1920,128]{1,0:T(8,128)} all-gather(f32[120,128]{1,0:T(8,128)S(1)} %select_maximum_fusion.1), channel_id=2, replica_groups=mesh['row'=32,'col'=16] {'col'}, dimensions={0}, use_global_device_ids=true | all-gather | bytes 1044480 | tf_op jit(solution)/shard_map/all_gather | solution.py:202
  86.9 0.0 collective-permute-done.3
  86.9 0.0 collective-permute-done.4
  86.9 0.0 collective-permute-done.5
  86.9 0.1 pad_maximum_fusion.mine
  87.1 0.0 copy-start
  87.1 1.9 %collective-permute-start.6 = (f32[16,264,128]{2,1,0:T(8,128)S(1)}, f32[16,264,128]{2,1,0:T(8,128)}, u32[]{:S(2)}, u32[]{:S(2)}) collective-permute-start(f32[16,264,128]{2,1,0:T(8,128)S(1)} %pad_maximum_fusion.mine), channel_id=1, source_target_pairs={{0,16},{16,0},{32,48},{48,32},{64,80},{80,64},{96,112},{112,96},{1... | collective-permute-start | bytes 6488072 | tf_op jit(solution)/shard_map/ppermute | solution.py:33
  89.0 0.6 pad_add_fusion.me
  89.7 3.7 %collective-permute-done.6.other = f32[16,264,128]{2,1,0:T(8,128)} collective-permute-done((f32[16,264,128]{2,1,0:T(8,128)S(1)}, f32[16,264,128]{2,1,0:T(8,128)}, u32[]{:S(2)}, u32[]{:S(2)}) %collective-permute-start.6) | collective-permute-done | bytes 2162720 | tf_op jit(solution)/shard_map/ppermute | solution.py:33
  93.3 0.0 copy-done
  93.3 8.3 %shard_map.46 = (s32[6,68]{1,0:T(8,128)}, bf16[68,128,256]{2,1,0:T(8,128)(2,1)}) custom-call(s32[3]{0:T(128)} %pad_add_fusion.me, f32[16,120,128]{2,1,0:T(8,128)} %bitcast.12, f32[16,264,128]{2,1,0:T(8,128)} %copy-done, f32[16,264,128]{2,1,0:T(8,128)} %collective-permute-done.6.other), custom_call_target="tpu_custom_call" | custom-call | tf_op jit(solution)/shard_map/pallas_call | solution.py:162
  101.7 0.0 all-gather.4.cloned.1.call-done
  101.7 4.8 %shard_map.47 = f32[512,512]{1,0:T(8,128)} custom-call(s32[6,68]{1,0:T(8,128)} %get-tuple-element.15.todo, f32[16,400,128]{2,1,0:T(8,128)} %bitcast.14, f32[16,120,128]{2,1,0:T(8,128)} %bitcast.13, bf16[68,128,256]{2,1,0:T(8,128)(2,1)} %get-tuple-element.16.staged), custom_call_target="tpu_custom_call" | custom-call | tf_op jit(solution)/shard_map/pallas_call | solution.py:181
  (1 shorter events, 0.0 us)
Async XLA Ops:
  6.5 95.1 %all-gather.4.cloned.1.call-start = ((), (), s32[]{:S(2)}) async-start(), calls=%async_computation | async-start | bytes 3481600 | tf_op jit(solution)/shard_map/all_gather | solution.py:198
  9.9 14.1 %collective-permute-start = (f32[264,128]{1,0:T(8,128)S(1)}, f32[264,128]{1,0:T(8,128)S(1)}, u32[]{:S(2)}, u32[]{:S(2)}) collective-permute-start(f32[264,128]{1,0:T(8,128)S(1)} %get-tuple-element.18), channel_id=1, source_target_pairs={{0,128},{16,144},{32,160},{48,176},{64,192},{80,208},{96,224},{112... | collective-permute-start | bytes 405512 | tf_op jit(solution)/shard_map/ppermute | solution.py:33
  17.7 8.4 %collective-permute-start.1 = (f32[264,128]{1,0:T(8,128)S(1)}, f32[264,128]{1,0:T(8,128)S(1)}, u32[]{:S(2)}, u32[]{:S(2)}) collective-permute-start(f32[264,128]{1,0:T(8,128)S(1)} %get-tuple-element.18), channel_id=1, source_target_pairs={{0,256},{16,272},{32,288},{48,304},{64,320},{80,336},{96,352},{112... | collective-permute-start | bytes 405512 | tf_op jit(solution)/shard_map/ppermute | solution.py:33
  19.6 8.1 %collective-permute-start.2 = (f32[264,128]{1,0:T(8,128)S(1)}, f32[264,128]{1,0:T(8,128)S(1)}, u32[]{:S(2)}, u32[]{:S(2)}) collective-permute-start(f32[264,128]{1,0:T(8,128)S(1)} %get-tuple-element.18), channel_id=1, source_target_pairs={{0,384},{16,400},{32,416},{48,432},{64,448},{80,464},{96,480},{112... | collective-permute-start | bytes 405512 | tf_op jit(solution)/shard_map/ppermute | solution.py:33
  27.8 59.1 %collective-permute-start.3 = (f32[4,264,128]{2,1,0:T(8,128)S(1)}, f32[4,264,128]{2,1,0:T(8,128)S(1)}, u32[]{:S(2)}, u32[]{:S(2)}) collective-permute-start(f32[4,264,128]{2,1,0:T(8,128)S(1)} %pad_maximum_fusion.1), channel_id=1, source_target_pairs={{0,32},{16,48},{32,64},{48,80},{64,96},{80,112},{96,0},{112,16},{1... | collective-permute-start | bytes 1622024 | tf_op jit(solution)/shard_map/ppermute | solution.py:33
  29.7 57.2 %collective-permute-start.4 = (f32[4,264,128]{2,1,0:T(8,128)S(1)}, f32[4,264,128]{2,1,0:T(8,128)S(1)}, u32[]{:S(2)}, u32[]{:S(2)}) collective-permute-start(f32[4,264,128]{2,1,0:T(8,128)S(1)} %pad_maximum_fusion.1), channel_id=1, source_target_pairs={{0,64},{16,80},{32,96},{48,112},{64,0},{80,16},{96,32},{112,48},{1... | collective-permute-start | bytes 1622024 | tf_op jit(solution)/shard_map/ppermute | solution.py:33
  33.1 53.8 %collective-permute-start.5 = (f32[4,264,128]{2,1,0:T(8,128)S(1)}, f32[4,264,128]{2,1,0:T(8,128)S(1)}, u32[]{:S(2)}, u32[]{:S(2)}) collective-permute-start(f32[4,264,128]{2,1,0:T(8,128)S(1)} %pad_maximum_fusion.1), channel_id=1, source_target_pairs={{0,96},{16,112},{32,0},{48,16},{64,32},{80,48},{96,64},{112,80},{1... | collective-permute-start | bytes 1622024 | tf_op jit(solution)/shard_map/ppermute | solution.py:33
  87.1 6.3 %copy-start = (f32[16,264,128]{2,1,0:T(8,128)}, f32[16,264,128]{2,1,0:T(8,128)S(1)}, u32[]{:S(2)}) copy-start(f32[16,264,128]{2,1,0:T(8,128)S(1)} %pad_maximum_fusion.mine) | copy-start | bytes 6488068
  87.1 6.3 %collective-permute-start.6 = (f32[16,264,128]{2,1,0:T(8,128)S(1)}, f32[16,264,128]{2,1,0:T(8,128)}, u32[]{:S(2)}, u32[]{:S(2)}) collective-permute-start(f32[16,264,128]{2,1,0:T(8,128)S(1)} %pad_maximum_fusion.mine), channel_id=1, source_target_pairs={{0,16},{16,0},{32,48},{48,32},{64,80},{80,64},{96,112},{112,96},{1... | collective-permute-start | bytes 6488072 | tf_op jit(solution)/shard_map/ppermute | solution.py:33
Sparse Core Ops, SparseCore 0:
  9.4 85.0 all-gather.3

commit v5 on v3

--- a/solution.py
+++ b/solution.py
@@ -91,7 +91,7 @@
     todo[5, 0] = count
 
 
-def product_kernel(todo, left, staged, out_ref, l_buf, r_buf, sem, r_sem):
+def product_kernel(todo, left, staged, product, out_ref, l_buf, r_buf, sem, r_sem, out_sem):
     steps = lax.div(todo[5, 0] + UNROLL - 1, UNROLL)
 
     def fetch(n):
@@ -130,6 +130,15 @@
         return carry
 
     lax.fori_loop(0, steps, multiply, 0)
+    bands = [pl.ds(i * BS, BS) for i in range(BR)]
+    copies = [
+        pltpu.make_async_copy(out_ref.at[band], product.at[band], out_sem.at[i])
+        for i, band in enumerate(bands)
+    ]
+    for copy in copies:
+        copy.start()
+    for copy in copies:
+        copy.wait()
 
 
 HBM = pl.BlockSpec(memory_space=pltpu.HBM)
@@ -163,12 +172,14 @@
         product_kernel,
         out_shape=jax.ShapeDtypeStruct((BR * BS, BC * BS), F32),
         in_specs=[SMEM, HBM, HBM],
-        out_specs=VMEM,
+        out_specs=HBM,
         scratch_shapes=[
+            pltpu.VMEM((BR * BS, BC * BS), F32),
             pltpu.VMEM((MOST + UNROLL, BS, BS), F32),
             pltpu.VMEM(staged.shape, staged.dtype),
             pltpu.SemaphoreType.DMA((MOST + UNROLL,)),
             pltpu.SemaphoreType.DMA((MOST // UNROLL,)),
+            pltpu.SemaphoreType.DMA((BR,)),
         ],
         compiler_params=ROOM,
     )(todo, left, staged)

time: 105 us -> 105 us (level)
  no operation moved by 1% of the time
where the time goes in v5:
time: 105 us
  blocking collectives  27 us (26%)
  starting transfers between devices  23.3 us (22%)
  waiting for transfers between devices  20.1 us (19%)
  between operations  14.2 us (14%)
  Pallas kernels  12.2 us (12%)
  other arithmetic  5 us (5%)
  local copies, waits for them, and re-layouts  2.94 us (3%)
    optimization_barrier x1, blocking collectives, per_device(): area, l_where = lax.optimization_barrier((area, l_where))  27 us
    ppermute x7, starting transfers between devices, along_row(): return lax.ppermute(x, 'row', pairs)  23.3 us
    all_gather x1, waiting for transfers between devices, per_device(): left = lax.all_gather(left_blocks.reshape(SLOTS * BS, BS), 'col', axis=0)  10.3 us
    ppermute x7, waiting for transfers between devices, along_row(): return lax.ppermute(x, 'row', pairs)  9.03 us
    pallas_call x1, Pallas kernels, matches(): pl.pallas_call(match_kernel, out_shape=[jax.ShapeDtypeStruct((6, MOST + U...  7.12 us
    pallas_call x1, Pallas kernels, products(): pl.pallas_call(product_kernel, out_shape=jax.ShapeDtypeStruct((BR * BS, B...  5.12 us
    unnamed x7, local copies, waits for them, and re-layouts  2.26 us
  transfers between devices with their start and end apart: 8, of which 4 were waited for; matrix products, arithmetic and copies ran while one was open for 7% of the time, Pallas kernels for 7%

profile of v5, /device:TPU:6, one launch (start us, length us, event | category | flops | bytes accessed | tf_op | source)
XLA Modules:
  0.0 104.8 jit_solution(4743529200044639672)
XLA Ops:
  6.5 0.7 all-gather.2.cloned.1.call-update
  7.3 0.7 convert_reduce_fusion
  8.0 0.1 convert_element_type.17
  8.0 0.9 fusion
  9.0 7.8 %collective-permute-start = (f32[264,128]{1,0:T(8,128)S(1)}, f32[264,128]{1,0:T(8,128)S(1)}, u32[]{:S(2)}, u32[]{:S(2)}) collective-permute-start(f32[264,128]{1,0:T(8,128)S(1)} %get-tuple-element.18), channel_id=1, source_target_pairs={{0,128},{16,144},{32,160},{48,176},{64,192},{80,208},{96,224},{112... | collective-permute-start | bytes 405512 | tf_op jit(solution)/shard_map/ppermute | solution.py:31
  16.7 1.9 %collective-permute-start.1 = (f32[264,128]{1,0:T(8,128)S(1)}, f32[264,128]{1,0:T(8,128)S(1)}, u32[]{:S(2)}, u32[]{:S(2)}) collective-permute-start(f32[264,128]{1,0:T(8,128)S(1)} %get-tuple-element.18), channel_id=1, source_target_pairs={{0,256},{16,272},{32,288},{48,304},{64,320},{80,336},{96,352},{112... | collective-permute-start | bytes 405512 | tf_op jit(solution)/shard_map/ppermute | solution.py:31
  18.7 2.8 %collective-permute-start.2 = (f32[264,128]{1,0:T(8,128)S(1)}, f32[264,128]{1,0:T(8,128)S(1)}, u32[]{:S(2)}, u32[]{:S(2)}) collective-permute-start(f32[264,128]{1,0:T(8,128)S(1)} %get-tuple-element.18), channel_id=1, source_target_pairs={{0,384},{16,400},{32,416},{48,432},{64,448},{80,464},{96,480},{112... | collective-permute-start | bytes 405512 | tf_op jit(solution)/shard_map/ppermute | solution.py:31
  21.4 0.0 collective-permute-done
  21.4 3.7 %collective-permute-done.1 = f32[264,128]{1,0:T(8,128)S(1)} collective-permute-done((f32[264,128]{1,0:T(8,128)S(1)}, f32[264,128]{1,0:T(8,128)S(1)}, u32[]{:S(2)}, u32[]{:S(2)}) %collective-permute-start.1) | collective-permute-done | bytes 135200 | tf_op jit(solution)/shard_map/ppermute | solution.py:31
  25.1 1.6 %collective-permute-done.2 = f32[264,128]{1,0:T(8,128)S(1)} collective-permute-done((f32[264,128]{1,0:T(8,128)S(1)}, f32[264,128]{1,0:T(8,128)S(1)}, u32[]{:S(2)}, u32[]{:S(2)}) %collective-permute-start.2) | collective-permute-done | bytes 135200 | tf_op jit(solution)/shard_map/ppermute | solution.py:31
  26.8 0.1 pad_maximum_fusion.1
  26.8 1.9 %collective-permute-start.3 = (f32[4,264,128]{2,1,0:T(8,128)S(1)}, f32[4,264,128]{2,1,0:T(8,128)S(1)}, u32[]{:S(2)}, u32[]{:S(2)}) collective-permute-start(f32[4,264,128]{2,1,0:T(8,128)S(1)} %pad_maximum_fusion.1), channel_id=1, source_target_pairs={{0,32},{16,48},{32,64},{48,80},{64,96},{80,112},{96,0},{112,16},{1... | collective-permute-start | bytes 1622024 | tf_op jit(solution)/shard_map/ppermute | solution.py:31
  28.8 3.4 %collective-permute-start.4 = (f32[4,264,128]{2,1,0:T(8,128)S(1)}, f32[4,264,128]{2,1,0:T(8,128)S(1)}, u32[]{:S(2)}, u32[]{:S(2)}) collective-permute-start(f32[4,264,128]{2,1,0:T(8,128)S(1)} %pad_maximum_fusion.1), channel_id=1, source_target_pairs={{0,64},{16,80},{32,96},{48,112},{64,0},{80,16},{96,32},{112,48},{1... | collective-permute-start | bytes 1622024 | tf_op jit(solution)/shard_map/ppermute | solution.py:31
  32.2 3.6 %collective-permute-start.5 = (f32[4,264,128]{2,1,0:T(8,128)S(1)}, f32[4,264,128]{2,1,0:T(8,128)}, u32[]{:S(2)}, u32[]{:S(2)}) collective-permute-start(f32[4,264,128]{2,1,0:T(8,128)S(1)} %pad_maximum_fusion.1), channel_id=1, source_target_pairs={{0,96},{16,112},{32,0},{48,16},{64,32},{80,48},{96,64},{112,80},{1... | collective-permute-start | bytes 1622024 | tf_op jit(solution)/shard_map/ppermute | solution.py:31
  35.8 1.3 %dynamic-slice = u32[1]{0:T(128)} dynamic-slice(u32[512]{0:T(512)} %constant.61, u32[]{:T(128)S(6)} %add.13), dynamic_slice_sizes={1} | dynamic-slice | bytes 12
  37.8 0.5 broadcast.21
  38.3 1.3 %reduce.7 = s32[2,2,2]{2,1,0:T(2,128)S(1)} reduce(s32[2,2,1,2]{3,2,1,0:T(1,128)} %param.5, s32[]{:T(128)} %broadcast.21), dimensions={2}, to_apply=%get-tuple-element.12.reduce_sub_computation.3 | reduce | bytes 68 | tf_op jit(solution)/shard_map/optimization_barrier | solution.py:192
  39.6 0.1 reshape.22
  39.7 0.2 dynamic-update-slice
  39.9 27.0 %all-reduce.1.l_where = s32[128]{0:T(128)} all-reduce(s32[128]{0:T(128)S(1)} %dynamic-update-slice), channel_id=1, replica_groups=mesh['row'=32,'col'=16] {'col'}, use_global_device_ids=true, to_apply=%add.1 | all-reduce | flops 128 | bytes 1024 | tf_op jit(solution)/shard_map/optimization_barrier | solution.py:195
  66.9 0.0 collective-permute-done.3
  66.9 0.0 collective-permute-done.4
  66.9 0.8 copy-done.1
  67.7 0.0 collective-permute-done.5
  67.7 1.4 %pad_maximum_fusion.mine = f32[16,264,128]{2,1,0:T(8,128)S(1)} fusion(f32[4,264,128]{2,1,0:T(8,128)} %collective-permute-done.5, f32[4,264,128]{2,1,0:T(8,128)} %copy-done.1, f32[4,264,128]{2,1,0:T(8,128)S(1)} %collective-permute-done.3, f32[4,264,128]{2,1,0:T(8,128)S(1)} %pad_maximum_fusion.1), kind=kLoop, calls=%fused_computation | loop fusion | flops 1622016 | bytes 4325376 | tf_op jit(solution)/shard_map/concatenate | solution.py:194
  69.1 1.9 %collective-permute-start.6 = (f32[16,264,128]{2,1,0:T(8,128)S(1)}, f32[16,264,128]{2,1,0:T(8,128)}, u32[]{:S(2)}, u32[]{:S(2)}) collective-permute-start(f32[16,264,128]{2,1,0:T(8,128)S(1)} %pad_maximum_fusion.mine), channel_id=1, source_target_pairs={{0,16},{16,0},{32,48},{48,32},{64,80},{80,64},{96,112},{112,96},{1... | collective-permute-start | bytes 6488072 | tf_op jit(solution)/shard_map/ppermute | solution.py:31
  71.1 0.6 pad_add_fusion.me
  71.7 3.7 %collective-permute-done.6.other = f32[16,264,128]{2,1,0:T(8,128)} collective-permute-done((f32[16,264,128]{2,1,0:T(8,128)S(1)}, f32[16,264,128]{2,1,0:T(8,128)}, u32[]{:S(2)}, u32[]{:S(2)}) %collective-permute-start.6) | collective-permute-done | bytes 2162720 | tf_op jit(solution)/shard_map/ppermute | solution.py:31
  75.4 0.0 copy-done
  75.4 7.1 %shard_map.46 = (s32[6,68]{1,0:T(8,128)}, bf16[68,128,256]{2,1,0:T(8,128)(2,1)}) custom-call(s32[3]{0:T(128)} %pad_add_fusion.me, s32[128]{0:T(128)} %all-reduce.1.l_where, f32[16,264,128]{2,1,0:T(8,128)} %copy-done, f32[16,264,128]{2,1,0:T(8,128)} %collective-permute-done.6.other), custom_call_target="tpu_custom_call" | custom-call | tf_op jit(solution)/shard_map/pallas_call | solution.py:153
  82.5 10.3 %all-gather.2.cloned.1.call-done.left = f32[16,512,128]{2,1,0:T(8,128)} async-done(((f32[1,512,128]{2,1,0:T(8,128)}), f32[16,512,128]{2,1,0:T(8,128)}) %all-gather.2.cloned.1.call-update) | async-done | bytes 4194320 | tf_op jit(solution)/shard_map/all_gather | solution.py:189
  92.8 5.1 %shard_map.47 = f32[512,512]{1,0:T(8,128)} custom-call(s32[6,68]{1,0:T(8,128)} %get-tuple-element.15.todo, f32[16,512,128]{2,1,0:T(8,128)} %all-gather.2.cloned.1.call-done.left, bf16[68,128,256]{2,1,0:T(8,128)(2,1)} %get-tuple-element.16.staged), custom_call_target="tpu_custom_call" | custom-call | tf_op jit(solution)/shard_map/pallas_call | solution.py:171
  (4 shorter events, 0.0 us)
Async XLA Ops:
  6.5 86.3 %all-gather.2.cloned.1.call-start = ((), (), s32[]{:S(2)}) async-start(), calls=%async_computation | async-start | bytes 4456448 | tf_op jit(solution)/shard_map/all_gather | solution.py:189
  9.0 12.5 %collective-permute-start = (f32[264,128]{1,0:T(8,128)S(1)}, f32[264,128]{1,0:T(8,128)S(1)}, u32[]{:S(2)}, u32[]{:S(2)}) collective-permute-start(f32[264,128]{1,0:T(8,128)S(1)} %get-tuple-element.18), channel_id=1, source_target_pairs={{0,128},{16,144},{32,160},{48,176},{64,192},{80,208},{96,224},{112... | collective-permute-start | bytes 405512 | tf_op jit(solution)/shard_map/ppermute | solution.py:31
  16.7 8.4 %collective-permute-start.1 = (f32[264,128]{1,0:T(8,128)S(1)}, f32[264,128]{1,0:T(8,128)S(1)}, u32[]{:S(2)}, u32[]{:S(2)}) collective-permute-start(f32[264,128]{1,0:T(8,128)S(1)} %get-tuple-element.18), channel_id=1, source_target_pairs={{0,256},{16,272},{32,288},{48,304},{64,320},{80,336},{96,352},{112... | collective-permute-start | bytes 405512 | tf_op jit(solution)/shard_map/ppermute | solution.py:31
  18.7 8.1 %collective-permute-start.2 = (f32[264,128]{1,0:T(8,128)S(1)}, f32[264,128]{1,0:T(8,128)S(1)}, u32[]{:S(2)}, u32[]{:S(2)}) collective-permute-start(f32[264,128]{1,0:T(8,128)S(1)} %get-tuple-element.18), channel_id=1, source_target_pairs={{0,384},{16,400},{32,416},{48,432},{64,448},{80,464},{96,480},{112... | collective-permute-start | bytes 405512 | tf_op jit(solution)/shard_map/ppermute | solution.py:31
  26.8 40.1 %collective-permute-start.3 = (f32[4,264,128]{2,1,0:T(8,128)S(1)}, f32[4,264,128]{2,1,0:T(8,128)S(1)}, u32[]{:S(2)}, u32[]{:S(2)}) collective-permute-start(f32[4,264,128]{2,1,0:T(8,128)S(1)} %pad_maximum_fusion.1), channel_id=1, source_target_pairs={{0,32},{16,48},{32,64},{48,80},{64,96},{80,112},{96,0},{112,16},{1... | collective-permute-start | bytes 1622024 | tf_op jit(solution)/shard_map/ppermute | solution.py:31
  28.8 38.2 %collective-permute-start.4 = (f32[4,264,128]{2,1,0:T(8,128)S(1)}, f32[4,264,128]{2,1,0:T(8,128)S(1)}, u32[]{:S(2)}, u32[]{:S(2)}) collective-permute-start(f32[4,264,128]{2,1,0:T(8,128)S(1)} %pad_maximum_fusion.1), channel_id=1, source_target_pairs={{0,64},{16,80},{32,96},{48,112},{64,0},{80,16},{96,32},{112,48},{1... | collective-permute-start | bytes 1622024 | tf_op jit(solution)/shard_map/ppermute | solution.py:31
  32.2 35.5 %collective-permute-start.5 = (f32[4,264,128]{2,1,0:T(8,128)S(1)}, f32[4,264,128]{2,1,0:T(8,128)}, u32[]{:S(2)}, u32[]{:S(2)}) collective-permute-start(f32[4,264,128]{2,1,0:T(8,128)S(1)} %pad_maximum_fusion.1), channel_id=1, source_target_pairs={{0,96},{16,112},{32,0},{48,16},{64,32},{80,48},{96,64},{112,80},{1... | collective-permute-start | bytes 1622024 | tf_op jit(solution)/shard_map/ppermute | solution.py:31
  66.9 0.8 copy-start.1
  69.1 6.3 %copy-start = (f32[16,264,128]{2,1,0:T(8,128)}, f32[16,264,128]{2,1,0:T(8,128)S(1)}, u32[]{:S(2)}) copy-start(f32[16,264,128]{2,1,0:T(8,128)S(1)} %pad_maximum_fusion.mine) | copy-start | bytes 6488068
  69.1 6.3 %collective-permute-start.6 = (f32[16,264,128]{2,1,0:T(8,128)S(1)}, f32[16,264,128]{2,1,0:T(8,128)}, u32[]{:S(2)}, u32[]{:S(2)}) collective-permute-start(f32[16,264,128]{2,1,0:T(8,128)S(1)} %pad_maximum_fusion.mine), channel_id=1, source_target_pairs={{0,16},{16,0},{32,48},{48,32},{64,80},{80,64},{96,112},{112,96},{1... | collective-permute-start | bytes 6488072 | tf_op jit(solution)/shard_map/ppermute | solution.py:31
Sparse Core Ops, SparseCore 0:
  9.4 83.3 all-gather.1

commit v6 on v3

--- a/solution.py
+++ b/solution.py
@@ -15,7 +15,7 @@
 SIDE = 4
 AREA = SIDE * SIDE
 SLOTS = STEPS * LCAP
-UNROLL = 4
+UNROLL = 8
 LIMIT = 60
 MOST = N_COL * SLOTS
 F32 = jnp.float32

time: 105 us -> 105 us (level)
  no operation moved by 1% of the time
where the time goes in v6:
time: 105 us; the launch traced here: 104 us
  blocking collectives  27 us (26%)
  starting transfers between devices  23.3 us (22%)
  waiting for transfers between devices  20.1 us (19%)
  between operations  14.2 us (14%)
  Pallas kernels  11.5 us (11%)
  other arithmetic  5.03 us (5%)
  local copies, waits for them, and re-layouts  2.94 us (3%)
    optimization_barrier x1, blocking collectives, per_device(): area, l_where = lax.optimization_barrier((area, l_where))  27 us
    ppermute x7, starting transfers between devices, along_row(): return lax.ppermute(x, 'row', pairs)  23.3 us
    all_gather x1, waiting for transfers between devices, per_device(): left = lax.all_gather(left_blocks.reshape(SLOTS * BS, BS), 'col', axis=0)  10.4 us
    ppermute x7, waiting for transfers between devices, along_row(): return lax.ppermute(x, 'row', pairs)  9 us
    pallas_call x1, Pallas kernels, matches(): pl.pallas_call(match_kernel, out_shape=[jax.ShapeDtypeStruct((6, MOST + U...  7.09 us
    pallas_call x1, Pallas kernels, products(): pl.pallas_call(product_kernel, out_shape=jax.ShapeDtypeStruct((BR * BS, B...  4.39 us
    unnamed x7, local copies, waits for them, and re-layouts  2.26 us
  transfers between devices with their start and end apart: 8, of which 4 were waited for; matrix products, arithmetic and copies ran while one was open for 7% of the time, Pallas kernels for 7%

profile of v6, /device:TPU:6, one launch (start us, length us, event | category | flops | bytes accessed | tf_op | source)
XLA Modules:
  0.0 104.1 jit_solution(2334038468767433334)
XLA Ops:
  6.5 0.7 all-gather.2.cloned.1.call-update
  7.3 0.7 convert_reduce_fusion
  8.0 0.1 convert_element_type.17
  8.0 0.9 fusion
  9.0 7.8 %collective-permute-start = (f32[264,128]{1,0:T(8,128)S(1)}, f32[264,128]{1,0:T(8,128)S(1)}, u32[]{:S(2)}, u32[]{:S(2)}) collective-permute-start(f32[264,128]{1,0:T(8,128)S(1)} %get-tuple-element.18), channel_id=1, source_target_pairs={{0,128},{16,144},{32,160},{48,176},{64,192},{80,208},{96,224},{112... | collective-permute-start | bytes 405512 | tf_op jit(solution)/shard_map/ppermute | solution.py:31
  16.7 1.9 %collective-permute-start.1 = (f32[264,128]{1,0:T(8,128)S(1)}, f32[264,128]{1,0:T(8,128)S(1)}, u32[]{:S(2)}, u32[]{:S(2)}) collective-permute-start(f32[264,128]{1,0:T(8,128)S(1)} %get-tuple-element.18), channel_id=1, source_target_pairs={{0,256},{16,272},{32,288},{48,304},{64,320},{80,336},{96,352},{112... | collective-permute-start | bytes 405512 | tf_op jit(solution)/shard_map/ppermute | solution.py:31
  18.7 2.8 %collective-permute-start.2 = (f32[264,128]{1,0:T(8,128)S(1)}, f32[264,128]{1,0:T(8,128)S(1)}, u32[]{:S(2)}, u32[]{:S(2)}) collective-permute-start(f32[264,128]{1,0:T(8,128)S(1)} %get-tuple-element.18), channel_id=1, source_target_pairs={{0,384},{16,400},{32,416},{48,432},{64,448},{80,464},{96,480},{112... | collective-permute-start | bytes 405512 | tf_op jit(solution)/shard_map/ppermute | solution.py:31
  21.4 0.0 collective-permute-done
  21.4 3.7 %collective-permute-done.1 = f32[264,128]{1,0:T(8,128)S(1)} collective-permute-done((f32[264,128]{1,0:T(8,128)S(1)}, f32[264,128]{1,0:T(8,128)S(1)}, u32[]{:S(2)}, u32[]{:S(2)}) %collective-permute-start.1) | collective-permute-done | bytes 135200 | tf_op jit(solution)/shard_map/ppermute | solution.py:31
  25.1 1.6 %collective-permute-done.2 = f32[264,128]{1,0:T(8,128)S(1)} collective-permute-done((f32[264,128]{1,0:T(8,128)S(1)}, f32[264,128]{1,0:T(8,128)S(1)}, u32[]{:S(2)}, u32[]{:S(2)}) %collective-permute-start.2) | collective-permute-done | bytes 135200 | tf_op jit(solution)/shard_map/ppermute | solution.py:31
  26.8 0.1 pad_maximum_fusion.1
  26.8 1.9 %collective-permute-start.3 = (f32[4,264,128]{2,1,0:T(8,128)S(1)}, f32[4,264,128]{2,1,0:T(8,128)S(1)}, u32[]{:S(2)}, u32[]{:S(2)}) collective-permute-start(f32[4,264,128]{2,1,0:T(8,128)S(1)} %pad_maximum_fusion.1), channel_id=1, source_target_pairs={{0,32},{16,48},{32,64},{48,80},{64,96},{80,112},{96,0},{112,16},{1... | collective-permute-start | bytes 1622024 | tf_op jit(solution)/shard_map/ppermute | solution.py:31
  28.8 3.4 %collective-permute-start.4 = (f32[4,264,128]{2,1,0:T(8,128)S(1)}, f32[4,264,128]{2,1,0:T(8,128)S(1)}, u32[]{:S(2)}, u32[]{:S(2)}) collective-permute-start(f32[4,264,128]{2,1,0:T(8,128)S(1)} %pad_maximum_fusion.1), channel_id=1, source_target_pairs={{0,64},{16,80},{32,96},{48,112},{64,0},{80,16},{96,32},{112,48},{1... | collective-permute-start | bytes 1622024 | tf_op jit(solution)/shard_map/ppermute | solution.py:31
  32.2 3.6 %collective-permute-start.5 = (f32[4,264,128]{2,1,0:T(8,128)S(1)}, f32[4,264,128]{2,1,0:T(8,128)}, u32[]{:S(2)}, u32[]{:S(2)}) collective-permute-start(f32[4,264,128]{2,1,0:T(8,128)S(1)} %pad_maximum_fusion.1), channel_id=1, source_target_pairs={{0,96},{16,112},{32,0},{48,16},{64,32},{80,48},{96,64},{112,80},{1... | collective-permute-start | bytes 1622024 | tf_op jit(solution)/shard_map/ppermute | solution.py:31
  35.8 1.3 %dynamic-slice = u32[1]{0:T(128)} dynamic-slice(u32[512]{0:T(512)} %constant.61, u32[]{:T(128)S(6)} %add.13), dynamic_slice_sizes={1} | dynamic-slice | bytes 12
  37.8 0.5 broadcast.21
  38.3 1.3 %reduce.7 = s32[2,2,2]{2,1,0:T(2,128)S(1)} reduce(s32[2,2,1,2]{3,2,1,0:T(1,128)} %param.5, s32[]{:T(128)} %broadcast.21), dimensions={2}, to_apply=%get-tuple-element.12.reduce_sub_computation.3 | reduce | bytes 68 | tf_op jit(solution)/shard_map/optimization_barrier | solution.py:181
  39.6 0.1 reshape.22
  39.7 0.2 dynamic-update-slice
  39.9 27.0 %all-reduce.1.l_where = s32[128]{0:T(128)} all-reduce(s32[128]{0:T(128)S(1)} %dynamic-update-slice), channel_id=1, replica_groups=mesh['row'=32,'col'=16] {'col'}, use_global_device_ids=true, to_apply=%add.1 | all-reduce | flops 128 | bytes 1024 | tf_op jit(solution)/shard_map/optimization_barrier | solution.py:184
  66.9 0.0 collective-permute-done.3
  66.9 0.0 collective-permute-done.4
  66.9 0.8 copy-done.1
  67.7 0.0 collective-permute-done.5
  67.7 1.4 %pad_maximum_fusion.mine = f32[16,264,128]{2,1,0:T(8,128)S(1)} fusion(f32[4,264,128]{2,1,0:T(8,128)} %collective-permute-done.5, f32[4,264,128]{2,1,0:T(8,128)} %copy-done.1, f32[4,264,128]{2,1,0:T(8,128)S(1)} %collective-permute-done.3, f32[4,264,128]{2,1,0:T(8,128)S(1)} %pad_maximum_fusion.1), kind=kLoop, calls=%fused_computation | loop fusion | flops 1622016 | bytes 4325376 | tf_op jit(solution)/shard_map/concatenate | solution.py:183
  69.1 1.9 %collective-permute-start.6 = (f32[16,264,128]{2,1,0:T(8,128)S(1)}, f32[16,264,128]{2,1,0:T(8,128)}, u32[]{:S(2)}, u32[]{:S(2)}) collective-permute-start(f32[16,264,128]{2,1,0:T(8,128)S(1)} %pad_maximum_fusion.mine), channel_id=1, source_target_pairs={{0,16},{16,0},{32,48},{48,32},{64,80},{80,64},{96,112},{112,96},{1... | collective-permute-start | bytes 6488072 | tf_op jit(solution)/shard_map/ppermute | solution.py:31
  71.1 0.7 pad_add_fusion.me
  71.7 3.7 %collective-permute-done.6.other = f32[16,264,128]{2,1,0:T(8,128)} collective-permute-done((f32[16,264,128]{2,1,0:T(8,128)S(1)}, f32[16,264,128]{2,1,0:T(8,128)}, u32[]{:S(2)}, u32[]{:S(2)}) %collective-permute-start.6) | collective-permute-done | bytes 2162720 | tf_op jit(solution)/shard_map/ppermute | solution.py:31
  75.4 0.0 copy-done
  75.4 7.1 %shard_map.46 = (s32[6,72]{1,0:T(8,128)}, bf16[72,128,256]{2,1,0:T(8,128)(2,1)}) custom-call(s32[3]{0:T(128)} %pad_add_fusion.me, s32[128]{0:T(128)} %all-reduce.1.l_where, f32[16,264,128]{2,1,0:T(8,128)} %copy-done, f32[16,264,128]{2,1,0:T(8,128)} %collective-permute-done.6.other), custom_call_target="tpu_custom_call" | custom-call | tf_op jit(solution)/shard_map/pallas_call | solution.py:144
  82.5 10.4 %all-gather.2.cloned.1.call-done.left = f32[16,512,128]{2,1,0:T(8,128)} async-done(((f32[1,512,128]{2,1,0:T(8,128)}), f32[16,512,128]{2,1,0:T(8,128)}) %all-gather.2.cloned.1.call-update) | async-done | bytes 4194320 | tf_op jit(solution)/shard_map/all_gather | solution.py:178
  92.8 4.4 %shard_map.47 = f32[512,512]{1,0:T(8,128)} custom-call(s32[6,72]{1,0:T(8,128)} %get-tuple-element.15.todo, f32[16,512,128]{2,1,0:T(8,128)} %all-gather.2.cloned.1.call-done.left, bf16[72,128,256]{2,1,0:T(8,128)(2,1)} %get-tuple-element.16.staged), custom_call_target="tpu_custom_call" | custom-call | tf_op jit(solution)/shard_map/pallas_call | solution.py:162
  (4 shorter events, 0.0 us)
Async XLA Ops:
  6.5 86.3 %all-gather.2.cloned.1.call-start = ((), (), s32[]{:S(2)}) async-start(), calls=%async_computation | async-start | bytes 4456448 | tf_op jit(solution)/shard_map/all_gather | solution.py:178
  9.0 12.5 %collective-permute-start = (f32[264,128]{1,0:T(8,128)S(1)}, f32[264,128]{1,0:T(8,128)S(1)}, u32[]{:S(2)}, u32[]{:S(2)}) collective-permute-start(f32[264,128]{1,0:T(8,128)S(1)} %get-tuple-element.18), channel_id=1, source_target_pairs={{0,128},{16,144},{32,160},{48,176},{64,192},{80,208},{96,224},{112... | collective-permute-start | bytes 405512 | tf_op jit(solution)/shard_map/ppermute | solution.py:31
  16.7 8.4 %collective-permute-start.1 = (f32[264,128]{1,0:T(8,128)S(1)}, f32[264,128]{1,0:T(8,128)S(1)}, u32[]{:S(2)}, u32[]{:S(2)}) collective-permute-start(f32[264,128]{1,0:T(8,128)S(1)} %get-tuple-element.18), channel_id=1, source_target_pairs={{0,256},{16,272},{32,288},{48,304},{64,320},{80,336},{96,352},{112... | collective-permute-start | bytes 405512 | tf_op jit(solution)/shard_map/ppermute | solution.py:31
  18.7 8.1 %collective-permute-start.2 = (f32[264,128]{1,0:T(8,128)S(1)}, f32[264,128]{1,0:T(8,128)S(1)}, u32[]{:S(2)}, u32[]{:S(2)}) collective-permute-start(f32[264,128]{1,0:T(8,128)S(1)} %get-tuple-element.18), channel_id=1, source_target_pairs={{0,384},{16,400},{32,416},{48,432},{64,448},{80,464},{96,480},{112... | collective-permute-start | bytes 405512 | tf_op jit(solution)/shard_map/ppermute | solution.py:31
  26.8 40.1 %collective-permute-start.3 = (f32[4,264,128]{2,1,0:T(8,128)S(1)}, f32[4,264,128]{2,1,0:T(8,128)S(1)}, u32[]{:S(2)}, u32[]{:S(2)}) collective-permute-start(f32[4,264,128]{2,1,0:T(8,128)S(1)} %pad_maximum_fusion.1), channel_id=1, source_target_pairs={{0,32},{16,48},{32,64},{48,80},{64,96},{80,112},{96,0},{112,16},{1... | collective-permute-start | bytes 1622024 | tf_op jit(solution)/shard_map/ppermute | solution.py:31
  28.8 38.2 %collective-permute-start.4 = (f32[4,264,128]{2,1,0:T(8,128)S(1)}, f32[4,264,128]{2,1,0:T(8,128)S(1)}, u32[]{:S(2)}, u32[]{:S(2)}) collective-permute-start(f32[4,264,128]{2,1,0:T(8,128)S(1)} %pad_maximum_fusion.1), channel_id=1, source_target_pairs={{0,64},{16,80},{32,96},{48,112},{64,0},{80,16},{96,32},{112,48},{1... | collective-permute-start | bytes 1622024 | tf_op jit(solution)/shard_map/ppermute | solution.py:31
  32.2 35.6 %collective-permute-start.5 = (f32[4,264,128]{2,1,0:T(8,128)S(1)}, f32[4,264,128]{2,1,0:T(8,128)}, u32[]{:S(2)}, u32[]{:S(2)}) collective-permute-start(f32[4,264,128]{2,1,0:T(8,128)S(1)} %pad_maximum_fusion.1), channel_id=1, source_target_pairs={{0,96},{16,112},{32,0},{48,16},{64,32},{80,48},{96,64},{112,80},{1... | collective-permute-start | bytes 1622024 | tf_op jit(solution)/shard_map/ppermute | solution.py:31
  66.9 0.8 copy-start.1
  69.1 6.3 %copy-start = (f32[16,264,128]{2,1,0:T(8,128)}, f32[16,264,128]{2,1,0:T(8,128)S(1)}, u32[]{:S(2)}) copy-start(f32[16,264,128]{2,1,0:T(8,128)S(1)} %pad_maximum_fusion.mine) | copy-start | bytes 6488068
  69.1 6.3 %collective-permute-start.6 = (f32[16,264,128]{2,1,0:T(8,128)S(1)}, f32[16,264,128]{2,1,0:T(8,128)}, u32[]{:S(2)}, u32[]{:S(2)}) collective-permute-start(f32[16,264,128]{2,1,0:T(8,128)S(1)} %pad_maximum_fusion.mine), channel_id=1, source_target_pairs={{0,16},{16,0},{32,48},{48,32},{64,80},{80,64},{96,112},{112,96},{1... | collective-permute-start | bytes 6488072 | tf_op jit(solution)/shard_map/ppermute | solution.py:31
Sparse Core Ops, SparseCore 0:
  9.4 83.3 all-gather.1
